TPU v7x, 32 devices: a whole 2x2x4 slice. The times are simulated.
32 devices in a mesh: groups: 2 (over y), tiles: 4 (over z), sub: 2 (over x), adj: 2 (over core).
Axes of the slice: x: 2, y: 2, z: 4, core: 2. Of those that a mesh axis runs over, the one named last changes fastest.
Arguments:
- innovation: float32 [128, 256], P(('groups', 'tiles'), 'sub'), parts along dimension 0, may hold values from -6 to 6
- cluster: int32 [128, 256], P(('groups', 'tiles'), 'sub'), parts along dimension 0, may hold values from 0 to 8
- kernel: float32 [36, 64, 256], P(None, 'tiles', 'sub'), may hold values from 0.2 to 1.5
- wind_x: float32 [36, 64, 256], P(None, 'tiles', 'sub'), may hold values from -0.24 to 0.24
- wind_y: float32 [36, 64, 256], P(None, 'tiles', 'sub'), may hold values from -0.24 to 0.24
- conv_strength: float32 [64, 256], P('tiles', 'sub'), may hold values from 0 to 0.9
- conv_matrix: float32 [36, 36], replicated, may hold values from 0 to 1, as said below
- margin_cell: int32 [6144, 8], P(('tiles', 'sub')), may hold values from 0 to 16383, as said below
- margin_weight: float32 [6144, 8], P(('tiles', 'sub')), may hold values from 0 to 1, as said below
Outputs:
- adjoint_field: float32 [16, 36, 64, 256], P(('groups', 'adj'), None, 'tiles', 'sub'), parts along dimension 0
- sensitivity: float32 [16, 6144], P(('groups', 'adj'), ('tiles', 'sub')), parts along dimension 0
There are 2 independent parts, one for each index of `groups`. A program takes and returns all parts, laid end to end along the dimension named above; an argument that names none is the same for every part. Nothing has to cross between parts.
Inputs may be any that keep to these rules, and one draw needn't show every extreme that they name: `conv_matrix`: entries are positive and every column sums to 1. `margin_cell`: state element e is owned by block b = e // 768, with t = b // 2 and s = b % 2; the column index of each of its cells lies in t * 16 - 16 to t * 16 + 2 * 16 - 1, taken modulo 64, and its row in s * 128 - 128 to s * 128 + 2 * 128 - 1 (within 0 to 255). `margin_weight`: each state element has 1 to 8 live slots first, element 0 all 8; the others have weight 0.
All inputs are finite; a program needn't handle non-finite values.
Results may differ from a plain program's by a relative error of at most 0.0003.
Values sent between devices are 32-bit elements; how exact they have to be, the bound alone decides.
A program may use at most 64 MiB of HBM per device.

v0:
```python
import jax
import jax.numpy as jnp
from jax import lax
from jax.sharding import PartitionSpec as P

ADJ = 8
NSTEP = 2


def shifted(value, axis, steps):
    count = lax.axis_size(axis)
    pairs = [(source, (source + steps) % count) for source in range(count)]
    return lax.ppermute(value, axis, pairs)


def passed_along(block, axis, distance):
    devices = range(lax.axis_size(axis))
    route = [(i - distance, i) for i in devices if i - distance in devices]
    return lax.ppermute(block, axis, route)


def extended(cells, sides, width, closed):
    for axis, dim in sides:
        count = lax.axis_size(axis)
        ends = count if closed else count - 1
        head = lax.slice_in_dim(cells, 0, width, axis=dim)
        tail = lax.slice_in_dim(cells, cells.shape[dim] - width, cells.shape[dim], axis=dim)
        cells = jnp.concatenate(
            [
                lax.ppermute(tail, axis, [(i, (i + 1) % count) for i in range(ends)]),
                cells,
                lax.ppermute(head, axis, [((i + 1) % count, i) for i in range(ends)]),
            ],
            axis=dim,
        )
    return cells


def convect(adjoint, strength, matrix):
    mixed = jnp.einsum("lk,alxy->akxy", matrix, adjoint, precision=lax.Precision.HIGHEST)
    return adjoint + strength * (mixed - adjoint)


def combine(center, east, west, north, south, east_rate, west_rate, north_rate, south_rate):
    rate_sum = 1.0 - east_rate + west_rate - north_rate + south_rate
    return (
        center * rate_sum
        + east_rate * east
        - west_rate * west
        + north_rate * north
        - south_rate * south
    )


def body(
    innovation,
    cluster,
    kernel,
    wind_x,
    wind_y,
    conv_strength,
    conv_matrix,
    margin_cell,
    margin_weight,
):
    width_x = kernel.shape[1]
    width_y = kernel.shape[2]
    per_device = ADJ // lax.axis_size("adj")
    cluster_ids = lax.axis_index("adj") * per_device + jnp.arange(per_device, dtype=jnp.int32)
    chosen = cluster[None] == cluster_ids[:, None, None]
    adjoint = jnp.where(chosen, innovation[None], 0.0)[:, None] * kernel[None]
    west_col = shifted(wind_x[:, -1:], "tiles", 1)
    south_row = passed_along(wind_y[:, :, -1:], "sub", 1)
    east_rate = jnp.maximum(wind_x, 0.0)
    west_rate = jnp.minimum(jnp.concatenate([west_col, wind_x[:, :-1]], axis=1), 0.0)
    north_rate = jnp.maximum(wind_y, 0.0)
    south_rate = jnp.minimum(jnp.concatenate([south_row, wind_y[:, :, :-1]], axis=2), 0.0)
    for step in range(NSTEP):
        adjoint = convect(adjoint, conv_strength, conv_matrix)
        edge_x = jnp.concatenate([adjoint[:, :, :1], adjoint[:, :, -1:]], axis=2)
        seams_x = extended(edge_x, (("tiles", 2),), 1, True)
        edge_y = jnp.concatenate([adjoint[:, :, :, :1], adjoint[:, :, :, -1:]], axis=3)
        seams_y = extended(edge_y, (("sub", 3),), 1, False)
        east = jnp.concatenate([adjoint[:, :, 1:], seams_x[:, :, 3:4]], axis=2)
        west = jnp.concatenate([seams_x[:, :, 0:1], adjoint[:, :, :-1]], axis=2)
        north = jnp.concatenate([adjoint[:, :, :, 1:], seams_y[:, :, :, 3:4]], axis=3)
        south = jnp.concatenate([seams_y[:, :, :, 0:1], adjoint[:, :, :, :-1]], axis=3)
        adjoint = combine(
            adjoint, east, west, north, south, east_rate, west_rate, north_rate, south_rate
        )
    surface = adjoint[:, 0]
    cycle_cells = extended(surface, (("tiles", 1),), width_x, True)
    rim_cells = extended(cycle_cells, (("sub", 2),), width_y, False)
    flat_surface = rim_cells.reshape(per_device, 9 * width_x * width_y)
    tile_pos = lax.axis_index("tiles")
    cross_pos = lax.axis_index("sub")
    cycle_length = width_x * lax.axis_size("tiles")
    cross_length = width_y * lax.axis_size("sub")
    column_x = margin_cell // cross_length
    row_y = margin_cell % cross_length
    local_x = (column_x - tile_pos * width_x + width_x + cycle_length) % cycle_length
    local_y = row_y - cross_pos * width_y + width_y
    local_index = local_x * (3 * width_y) + local_y
    values = jnp.take(flat_surface, local_index.reshape(-1), axis=1).reshape(
        per_device, margin_cell.shape[0], margin_cell.shape[1]
    )
    sensed = jnp.sum(margin_weight[None] * values, axis=2)
    return (adjoint, sensed)


def solution(mesh):
    in_specs = (
        P(("groups", "tiles"), "sub"),
        P(("groups", "tiles"), "sub"),
        P(None, "tiles", "sub"),
        P(None, "tiles", "sub"),
        P(None, "tiles", "sub"),
        P("tiles", "sub"),
        P(),
        P(("tiles", "sub"), None),
        P(("tiles", "sub"), None),
    )
    out_specs = (P(("groups", "adj"), None, "tiles", "sub"), P(("groups", "adj"), ("tiles", "sub")))
    return jax.shard_map(body, mesh=mesh, in_specs=in_specs, out_specs=out_specs, check_vma=False)
```

profile of v0, /device:TPU:0, one launch (start us, length us, event | category | flops | bytes accessed | tf_op | source)
XLA Modules:
  0.0 118.1 jit_solution(2258256967415636589)
XLA Ops:
  2.5 2.2 %multiply_add_fusion = f32[4,36,16,128]{3,1,2,0:T(8,128)S(1)} fusion(f32[16,128]{1,0:T(8,128)} %param.14, f32[36,16,128]{2,0,1:T(8,128)S(1)} %copy.36, f32[4,16,128]{2,1,0:T(8,128)S(1)} %compare_select_fusion.2, f32[36,36]{1,0:T(8,128)S(1)} %copy-done), kind=kOutput, calls=%fused_computation.4 | convolution fusion | flops 128876544 | bytes 1520704 | tf_op jit(solution)/shard_map/lk,alxy->akxy/dot_general | solution.py:40
  5.4 5.0 %collective-permute-start.2 = (f32[4,36,1,128]{3,1,2,0:T(8,128)}, f32[4,36,1,128]{3,1,2,0:T(8,128)S(1)}, u32[]{:S(2)}, u32[]{:S(2)}) collective-permute-start(f32[4,36,1,128]{3,1,2,0:T(8,128)} %get-tuple-element.26), channel_id=1, source_target_pairs={{4,0},{8,4},{12,8},{0,12},{5,1},{9,5},{13,9},{1,13},{6,2},{10,6},{... | collective-permute-start | bytes 221192 | tf_op jit(solution)/shard_map/ppermute | solution.py:32
  10.5 1.5 %fusion.58 = (f32[4,36,16,1]{3,1,2,0:T(8,128)S(1)}, f32[4,36,16,1]{3,1,2,0:T(8,128)}) fusion(f32[4,36,16,128]{3,1,2,0:T(8,128)S(1)} %multiply_add_fusion), kind=kLoop, calls=%fused_computation.83 | loop fusion | bytes 36864 | tf_op jit(solution)/shard_map/slice | solution.py:82
  12.0 1.9 %copy.42 = f32[4,36,16,1]{1,2,3,0:T(8,128)S(1)} copy(f32[4,36,16,1]{3,1,2,0:T(8,128)} %get-tuple-element.22) | data formatting | bytes 18432 | tf_op jit(solution)/shard_map/slice | solution.py:82
  13.9 1.3 %collective-permute-start.4 = (f32[4,36,16,1]{1,2,3,0:T(8,128)S(1)}, f32[4,36,16,1]{1,2,3,0:T(8,128)S(1)}, u32[]{:S(2)}, u32[]{:S(2)}) collective-permute-start(f32[4,36,16,1]{1,2,3,0:T(8,128)S(1)} %copy.42), channel_id=1, source_target_pairs={{2,0},{3,1},{6,4},{7,5},{10,8},{11,9},{14,12},{15,13},{18,16},{19,... | collective-permute-start | bytes 27656 | tf_op jit(solution)/shard_map/ppermute | solution.py:32
  15.7 4.5 %collective-permute-start.5 = (f32[4,36,16,1]{1,2,3,0:T(8,128)S(1)}, f32[4,36,16,1]{1,2,3,0:T(8,128)S(1)}, u32[]{:S(2)}, u32[]{:S(2)}) collective-permute-start(f32[4,36,16,1]{1,2,3,0:T(8,128)S(1)} %copy.45), channel_id=1, source_target_pairs={{0,2},{1,3},{4,6},{5,7},{8,10},{9,11},{12,14},{13,15},{16,18},{17,... | collective-permute-start | bytes 27656 | tf_op jit(solution)/shard_map/ppermute | solution.py:30
  20.5 1.3 %collective-permute-start.1 = (f32[36,16,1]{2,1,0:T(8,128)S(1)}, f32[36,16,1]{2,1,0:T(8,128)S(1)}, u32[]{:S(2)}, u32[]{:S(2)}) collective-permute-start(f32[36,16,1]{2,1,0:T(8,128)S(1)} %slice.65), channel_id=1, source_target_pairs={{0,2},{1,3},{4,6},{5,7},{8,10},{9,11},{12,14},{13,15},{16,18},{17,... | collective-permute-start | bytes 6920 | tf_op jit(solution)/shard_map/ppermute | solution.py:19
  21.8 1.6 %fusion.61 = (f32[4,36,15,128]{3,1,2,0:T(8,128)}, f32[4,36,15,128]{3,1,2,0:T(8,128)}) fusion(f32[4,36,16,128]{3,1,2,0:T(8,128)S(1)} %multiply_add_fusion), kind=kLoop, calls=%fused_computation.86 | loop fusion | bytes 4423680 | tf_op jit(solution)/shard_map/slice | solution.py:85
  23.5 1.9 %fusion.59 = (f32[4,36,16,127]{3,1,2,0:T(8,128)}, f32[4,36,16,127]{3,1,2,0:T(8,128)}) fusion(f32[4,36,16,128]{3,1,2,0:T(8,128)S(1)} %multiply_add_fusion), kind=kLoop, calls=%fused_computation.84 | loop fusion | bytes 4681728 | tf_op jit(solution)/shard_map/slice | solution.py:87
  26.5 1.6 %copy.43 = f32[4,36,16,1]{3,1,2,0:T(8,128)} copy(f32[4,36,16,1]{1,2,3,0:T(8,128)S(1)} %collective-permute-done.4) | data formatting | bytes 18432 | tf_op jit(solution)/shard_map/ppermute | solution.py:32
  28.2 1.7 %copy.46 = f32[4,36,16,1]{3,1,2,0:T(8,128)} copy(f32[4,36,16,1]{1,2,3,0:T(8,128)S(1)} %collective-permute-done.5) | data formatting | bytes 18432 | tf_op jit(solution)/shard_map/ppermute | solution.py:30
  30.6 1.3 %subtract_add_fusion = (f32[36,16,128]{2,1,0:T(8,128)S(1)}, f32[36,16,128]{2,1,0:T(8,128)S(1)}, f32[36,16,128]{2,1,0:T(8,128)S(1)}, f32[36,16,128]{2,1,0:T(8,128)S(1)}, f32[36,16,128]{2,1,0:T(8,128)S(1)}) fusion(f32[36,16,128]{2,1,0:T(8,128)S(1)} %copy-done.9, f32[36,16,128]{2,1,0:T(8,128)S(1)} %copy-done.8, f32[36,15,128]{2,1,0:T(8,128)S(1)} %bitcast.37, ...), kind=kLoop, calls=%fused_computation.49 | loop fusion | flops 737280 | bytes 2654208 | tf_op jit(solution)/shard_map/add | solution.py:45
  34.0 6.2 %fusion.6 = f32[4,36,16,128]{3,1,2,0:T(8,128)S(1)} fusion(f32[4,36,1,128]{3,1,2,0:T(8,128)S(1)} %collective-permute-done.2, f32[4,36,15,128]{3,1,2,0:T(8,128)} %get-tuple-element.28, f32[4,36,15,128]{3,1,2,0:T(8,128)} %get-tuple-element.27, f32[4,36,1,128]{3,1,2,0:T(8,128)S(1)} %collective-permute-done.3, f32[4,36,16,1]{3,1,2,0:T(8,128)S(1)} %copy-done.3, ...), kind=kOutput, calls=%fused_computation.11 | convolution fusion | flops 135954432 | bytes 8565824 | tf_op jit(solution)/shard_map/lk,alxy->akxy/dot_general | solution.py:40
  41.0 1.5 %fusion.54 = (f32[4,36,16,1]{3,1,2,0:T(8,128)S(1)}, f32[4,36,16,1]{3,1,2,0:T(8,128)}) fusion(f32[4,36,16,128]{3,1,2,0:T(8,128)S(1)} %fusion.6), kind=kLoop, calls=%fused_computation.79 | loop fusion | bytes 36864 | tf_op jit(solution)/shard_map/slice | solution.py:82
  42.4 1.9 %fusion.55 = (f32[4,36,16,127]{3,1,2,0:T(8,128)}, f32[4,36,16,127]{3,1,2,0:T(8,128)}) fusion(f32[4,36,16,128]{3,1,2,0:T(8,128)S(1)} %fusion.6), kind=kLoop, calls=%fused_computation.80 | loop fusion | bytes 4681728 | tf_op jit(solution)/shard_map/slice | solution.py:87
  44.4 3.8 %collective-permute-start.6 = (f32[4,36,1,128]{3,1,2,0:T(8,128)}, f32[4,36,1,128]{3,1,2,0:T(8,128)S(1)}, u32[]{:S(2)}, u32[]{:S(2)}) collective-permute-start(f32[4,36,1,128]{3,1,2,0:T(8,128)} %get-tuple-element.18), channel_id=1, source_target_pairs={{4,0},{8,4},{12,8},{0,12},{5,1},{9,5},{13,9},{1,13},{6,2},{10,6},{... | collective-permute-start | bytes 221192 | tf_op jit(solution)/shard_map/ppermute | solution.py:32
  48.2 1.9 %copy.48 = f32[4,36,16,1]{1,2,3,0:T(8,128)S(1)} copy(f32[4,36,16,1]{3,1,2,0:T(8,128)} %get-tuple-element.14) | data formatting | bytes 18432 | tf_op jit(solution)/shard_map/slice | solution.py:82
  50.0 1.3 %collective-permute-start.8 = (f32[4,36,16,1]{1,2,3,0:T(8,128)S(1)}, f32[4,36,16,1]{1,2,3,0:T(8,128)S(1)}, u32[]{:S(2)}, u32[]{:S(2)}) collective-permute-start(f32[4,36,16,1]{1,2,3,0:T(8,128)S(1)} %copy.48), channel_id=1, source_target_pairs={{2,0},{3,1},{6,4},{7,5},{10,8},{11,9},{14,12},{15,13},{18,16},{19,... | collective-permute-start | bytes 27656 | tf_op jit(solution)/shard_map/ppermute | solution.py:32
  52.5 4.7 %collective-permute-start.9 = (f32[4,36,16,1]{1,2,3,0:T(8,128)}, f32[4,36,16,1]{1,2,3,0:T(8,128)S(1)}, u32[]{:S(2)}, u32[]{:S(2)}) collective-permute-start(f32[4,36,16,1]{1,2,3,0:T(8,128)} %copy.50), channel_id=1, source_target_pairs={{0,2},{1,3},{4,6},{5,7},{8,10},{9,11},{12,14},{13,15},{16,18},{17,... | collective-permute-start | bytes 27656 | tf_op jit(solution)/shard_map/ppermute | solution.py:30
  57.2 1.6 %fusion.57 = (f32[4,36,15,128]{3,1,2,0:T(8,128)}, f32[4,36,15,128]{3,1,2,0:T(8,128)}) fusion(f32[4,36,16,128]{3,1,2,0:T(8,128)S(1)} %fusion.6), kind=kLoop, calls=%fused_computation.82 | loop fusion | bytes 4423680 | tf_op jit(solution)/shard_map/slice | solution.py:85
  58.8 1.6 %copy.49 = f32[4,36,16,1]{3,1,2,0:T(8,128)} copy(f32[4,36,16,1]{1,2,3,0:T(8,128)S(1)} %collective-permute-done.8) | data formatting | bytes 18432 | tf_op jit(solution)/shard_map/ppermute | solution.py:32
  60.5 1.7 %copy.51 = f32[4,36,16,1]{3,1,2,0:T(8,128)} copy(f32[4,36,16,1]{1,2,3,0:T(8,128)S(1)} %collective-permute-done.9) | data formatting | bytes 18432 | tf_op jit(solution)/shard_map/ppermute | solution.py:30
  62.2 4.7 %fusion.33 = f32[4,36,16,128]{3,1,2,0:T(8,128)S(1)} fusion(f32[4,36,1,128]{3,1,2,0:T(8,128)S(1)} %collective-permute-done.6, f32[4,36,15,128]{3,1,2,0:T(8,128)} %get-tuple-element.20, f32[4,36,15,128]{3,1,2,0:T(8,128)} %get-tuple-element.19, f32[4,36,1,128]{3,1,2,0:T(8,128)S(1)} %collective-permute-done.7, f32[4,36,16,1]{3,1,2,0:T(8,128)} %copy.49, ...), kind=kLoop, calls=%fused_computation.34 | loop fusion | flops 3833856 | bytes 8552448 | tf_op jit(solution)/shard_map/sub | solution.py:47
  66.9 3.9 %collective-permute-start.11 = (f32[4,16,128]{2,1,0:T(8,128)S(1)}, f32[4,16,128]{2,1,0:T(8,128)S(1)}, u32[]{:S(2)}, u32[]{:S(2)}) collective-permute-start(f32[4,16,128]{2,1,0:T(8,128)S(1)} %bitcast.38), channel_id=1, source_target_pairs={{4,0},{8,4},{12,8},{0,12},{5,1},{9,5},{13,9},{1,13},{6,2},{10,6},{... | collective-permute-start | bytes 98312 | tf_op jit(solution)/shard_map/ppermute | solution.py:32
  70.8 1.6 %collective-permute-done.11 = f32[4,16,128]{2,1,0:T(8,128)S(1)} collective-permute-done((f32[4,16,128]{2,1,0:T(8,128)S(1)}, f32[4,16,128]{2,1,0:T(8,128)S(1)}, u32[]{:S(2)}, u32[]{:S(2)}) %collective-permute-start.11) | collective-permute-done | bytes 32800 | tf_op jit(solution)/shard_map/ppermute | solution.py:32
  72.4 4.1 %collective-permute-done.10 = f32[4,16,128]{2,1,0:T(8,128)S(1)} collective-permute-done((f32[4,16,128]{2,1,0:T(8,128)S(1)}, f32[4,16,128]{2,1,0:T(8,128)S(1)}, u32[]{:S(2)}, u32[]{:S(2)}) %collective-permute-start.10) | collective-permute-done | bytes 32800 | tf_op jit(solution)/shard_map/ppermute | solution.py:30
  76.5 1.3 %collective-permute-start.13 = (f32[4,48,128]{2,1,0:T(8,128)S(1)}, f32[4,48,128]{2,1,0:T(8,128)S(1)}, u32[]{:S(2)}, u32[]{:S(2)}) collective-permute-start(f32[4,48,128]{2,1,0:T(8,128)S(1)} %pad_maximum_fusion.1), channel_id=1, source_target_pairs={{2,0},{3,1},{6,4},{7,5},{10,8},{11,9},{14,12},{15,13},{18,16},{19,... | collective-permute-start | bytes 294920 | tf_op jit(solution)/shard_map/ppermute | solution.py:32
  77.8 4.6 %collective-permute-start.12 = (f32[4,48,128]{2,1,0:T(8,128)S(1)}, f32[4,48,128]{2,1,0:T(8,128)S(1)}, u32[]{:S(2)}, u32[]{:S(2)}) collective-permute-start(f32[4,48,128]{2,1,0:T(8,128)S(1)} %pad_maximum_fusion.1), channel_id=1, source_target_pairs={{0,2},{1,3},{4,6},{5,7},{8,10},{9,11},{12,14},{13,15},{16,18},{17,... | collective-permute-start | bytes 294920 | tf_op jit(solution)/shard_map/ppermute | solution.py:30
  84.8 5.7 %copy.62 = f32[4,48,384]{0,2,1:T(8,128)} copy(f32[4,48,384]{2,1,0:T(8,128)S(1)} %pad_maximum_fusion) | data formatting | bytes 589824 | tf_op jit(solution)/shard_map/reshape | solution.py:94
  90.5 19.8 %gather_fusion = f32[6144,4]{1,0:T(8,128)S(1)} fusion(f32[4,18432]{0,1:T(8,128)} %bitcast.35, s32[6144]{0:T(1024)S(1)} %broadcast_clamp_fusion), kind=kCustom, calls=%fused_computation | custom fusion | bytes 221184 | tf_op jit(solution)/shard_map/jit(_take)/gather | solution.py:104
  110.2 6.1 %fusion.1 = f32[4,768]{0,1:T(8,128)} fusion(f32[6144,4]{1,0:T(8,128)S(1)} %gather_fusion, f32[768,8]{1,0:T(8,128)} %copy.52, pred[768,8]{1,0:T(8,128)(4,1)S(1)} %copy.53), kind=kLoop, calls=%fused_computation.3 | loop fusion | flops 70656 | bytes 141312 | tf_op jit(solution)/shard_map/reduce_sum | solution.py:107
  116.4 1.7 %copy.57 = f32[4,768]{1,0:T(4,128)} copy(f32[4,768]{0,1:T(8,128)} %fusion.1) | data formatting | bytes 24576
  (73 shorter events, 11.5 us)
Async XLA Ops:
  0.6 1.9 %copy-start = (f32[36,36]{1,0:T(8,128)S(1)}, f32[36,36]{1,0:T(8,128)}, u32[]{:S(2)}) copy-start(f32[36,36]{1,0:T(8,128)} %param.15) | copy-start | bytes 15556
  5.4 27.0 %collective-permute-start.2 = (f32[4,36,1,128]{3,1,2,0:T(8,128)}, f32[4,36,1,128]{3,1,2,0:T(8,128)S(1)}, u32[]{:S(2)}, u32[]{:S(2)}) collective-permute-start(f32[4,36,1,128]{3,1,2,0:T(8,128)} %get-tuple-element.26), channel_id=1, source_target_pairs={{4,0},{8,4},{12,8},{0,12},{5,1},{9,5},{13,9},{1,13},{6,2},{10,6},{... | collective-permute-start | bytes 221192 | tf_op jit(solution)/shard_map/ppermute | solution.py:32
  12.0 8.3 %copy-start.9 = (f32[36,16,128]{2,1,0:T(8,128)S(1)}, f32[36,16,128]{2,1,0:T(8,128)}, u32[]{:S(2)}) copy-start(f32[36,16,128]{2,1,0:T(8,128)} %param.12) | copy-start | bytes 884740
  12.0 8.4 %copy-start.8 = (f32[36,16,128]{2,1,0:T(8,128)S(1)}, f32[36,16,128]{2,1,0:T(8,128)}, u32[]{:S(2)}) copy-start(f32[36,16,128]{2,1,0:T(8,128)} %param.13) | copy-start | bytes 884740
  13.9 12.5 %collective-permute-start.4 = (f32[4,36,16,1]{1,2,3,0:T(8,128)S(1)}, f32[4,36,16,1]{1,2,3,0:T(8,128)S(1)}, u32[]{:S(2)}, u32[]{:S(2)}) collective-permute-start(f32[4,36,16,1]{1,2,3,0:T(8,128)S(1)} %copy.42), channel_id=1, source_target_pairs={{2,0},{3,1},{6,4},{7,5},{10,8},{11,9},{14,12},{15,13},{18,16},{19,... | collective-permute-start | bytes 27656 | tf_op jit(solution)/shard_map/ppermute | solution.py:32
  15.7 12.4 %collective-permute-start.5 = (f32[4,36,16,1]{1,2,3,0:T(8,128)S(1)}, f32[4,36,16,1]{1,2,3,0:T(8,128)S(1)}, u32[]{:S(2)}, u32[]{:S(2)}) collective-permute-start(f32[4,36,16,1]{1,2,3,0:T(8,128)S(1)} %copy.45), channel_id=1, source_target_pairs={{0,2},{1,3},{4,6},{5,7},{8,10},{9,11},{12,14},{13,15},{16,18},{17,... | collective-permute-start | bytes 27656 | tf_op jit(solution)/shard_map/ppermute | solution.py:30
  20.3 9.5 %collective-permute-start = (f32[36,1,128]{2,1,0:T(1,128)S(1)}, f32[36,1,128]{2,1,0:T(1,128)S(1)}, u32[]{:S(2)}, u32[]{:S(2)}) collective-permute-start(f32[36,1,128]{2,1,0:T(1,128)S(1)} %slice.63), channel_id=1, source_target_pairs={{0,4},{4,8},{8,12},{12,0},{1,5},{5,9},{9,13},{13,1},{2,6},{6,10},{... | collective-permute-start | bytes 55304 | tf_op jit(solution)/shard_map/ppermute | solution.py:13
  20.5 9.3 %collective-permute-start.1 = (f32[36,16,1]{2,1,0:T(8,128)S(1)}, f32[36,16,1]{2,1,0:T(8,128)S(1)}, u32[]{:S(2)}, u32[]{:S(2)}) collective-permute-start(f32[36,16,1]{2,1,0:T(8,128)S(1)} %slice.65), channel_id=1, source_target_pairs={{0,2},{1,3},{4,6},{5,7},{8,10},{9,11},{12,14},{13,15},{16,18},{17,... | collective-permute-start | bytes 6920 | tf_op jit(solution)/shard_map/ppermute | solution.py:19
  23.5 1.9 %copy-start.12 = (s32[768,8]{0,1:T(8,128)S(1)}, s32[768,8]{0,1:T(8,128)}, u32[]{:S(2)}) copy-start(s32[768,8]{0,1:T(8,128)} %param.16) | copy-start | bytes 73732
  23.5 3.0 %copy-start.11 = (f32[4,36,1,128]{3,1,2,0:T(8,128)S(1)}, f32[4,36,1,128]{3,1,2,0:T(8,128)}, u32[]{:S(2)}) copy-start(f32[4,36,1,128]{3,1,2,0:T(8,128)} %get-tuple-element.25) | copy-start | bytes 221188
  26.4 6.3 %collective-permute-start.3 = (f32[4,36,1,128]{3,1,2,0:T(8,128)S(1)}, f32[4,36,1,128]{3,1,2,0:T(8,128)S(1)}, u32[]{:S(2)}, u32[]{:S(2)}) collective-permute-start(f32[4,36,1,128]{3,1,2,0:T(8,128)S(1)} %copy-done.11), channel_id=1, source_target_pairs={{0,4},{4,8},{8,12},{12,0},{1,5},{5,9},{9,13},{13,1},{2,6},{6,10},{... | collective-permute-start | bytes 221192 | tf_op jit(solution)/shard_map/ppermute | solution.py:30
  29.8 0.7 copy-start.10
  30.6 2.2 %copy-start.3 = (f32[4,36,16,1]{3,1,2,0:T(8,128)S(1)}, f32[4,36,16,1]{3,1,2,0:T(8,128)}, u32[]{:S(2)}) copy-start(f32[4,36,16,1]{3,1,2,0:T(8,128)} %copy.43) | copy-start | bytes 27652
  30.6 2.2 %copy-start.4 = (f32[4,36,16,1]{3,1,2,0:T(8,128)S(1)}, f32[4,36,16,1]{3,1,2,0:T(8,128)}, u32[]{:S(2)}) copy-start(f32[4,36,16,1]{3,1,2,0:T(8,128)} %copy.46) | copy-start | bytes 27652
  31.9 1.5 %copy-start.2 = (f32[4,36,16,127]{3,1,2,0:T(8,128)S(1)}, f32[4,36,16,127]{3,1,2,0:T(8,128)}, u32[]{:S(2)}) copy-start(f32[4,36,16,127]{3,1,2,0:T(8,128)} %get-tuple-element.24) | copy-start | bytes 3511300
  32.0 2.0 %copy-start.1 = (f32[4,36,16,127]{3,1,2,0:T(8,128)S(1)}, f32[4,36,16,127]{3,1,2,0:T(8,128)}, u32[]{:S(2)}) copy-start(f32[4,36,16,127]{3,1,2,0:T(8,128)} %get-tuple-element.23) | copy-start | bytes 3511300
  32.0 2.0 %copy-start.15 = (f32[16,128]{1,0:T(8,128)S(1)}, f32[16,128]{1,0:T(8,128)}, u32[]{:S(2)}) copy-start(f32[16,128]{1,0:T(8,128)} %param.14) | copy-start | bytes 24580
  32.2 8.0 %copy-start.5 = (f32[36,16,128]{2,0,1:T(8,128)}, f32[36,16,128]{2,0,1:T(8,128)S(1)}, u32[]{:S(2)}) copy-start(f32[36,16,128]{2,0,1:T(8,128)S(1)} %copy.40) | copy-start | bytes 884740
  32.3 7.9 %copy-start.6 = (f32[36,16,128]{2,0,1:T(8,128)}, f32[36,16,128]{2,0,1:T(8,128)S(1)}, u32[]{:S(2)}) copy-start(f32[36,16,128]{2,0,1:T(8,128)S(1)} %copy.39) | copy-start | bytes 884740
  32.4 7.8 %copy-start.7 = (f32[36,16,128]{2,0,1:T(8,128)}, f32[36,16,128]{2,0,1:T(8,128)S(1)}, u32[]{:S(2)}) copy-start(f32[36,16,128]{2,0,1:T(8,128)S(1)} %copy.38) | copy-start | bytes 884740
  44.4 17.8 %collective-permute-start.6 = (f32[4,36,1,128]{3,1,2,0:T(8,128)}, f32[4,36,1,128]{3,1,2,0:T(8,128)S(1)}, u32[]{:S(2)}, u32[]{:S(2)}) collective-permute-start(f32[4,36,1,128]{3,1,2,0:T(8,128)} %get-tuple-element.18), channel_id=1, source_target_pairs={{4,0},{8,4},{12,8},{0,12},{5,1},{9,5},{13,9},{1,13},{6,2},{10,6},{... | collective-permute-start | bytes 221192 | tf_op jit(solution)/shard_map/ppermute | solution.py:32
  48.2 14.0 %collective-permute-start.7 = (f32[4,36,1,128]{3,1,2,0:T(8,128)}, f32[4,36,1,128]{3,1,2,0:T(8,128)S(1)}, u32[]{:S(2)}, u32[]{:S(2)}) collective-permute-start(f32[4,36,1,128]{3,1,2,0:T(8,128)} %get-tuple-element.17), channel_id=1, source_target_pairs={{0,4},{4,8},{8,12},{12,0},{1,5},{5,9},{9,13},{13,1},{2,6},{6,10},{... | collective-permute-start | bytes 221192 | tf_op jit(solution)/shard_map/ppermute | solution.py:30
  50.0 8.8 %collective-permute-start.8 = (f32[4,36,16,1]{1,2,3,0:T(8,128)S(1)}, f32[4,36,16,1]{1,2,3,0:T(8,128)S(1)}, u32[]{:S(2)}, u32[]{:S(2)}) collective-permute-start(f32[4,36,16,1]{1,2,3,0:T(8,128)S(1)} %copy.48), channel_id=1, source_target_pairs={{2,0},{3,1},{6,4},{7,5},{10,8},{11,9},{14,12},{15,13},{18,16},{19,... | collective-permute-start | bytes 27656 | tf_op jit(solution)/shard_map/ppermute | solution.py:32
  52.5 8.0 %collective-permute-start.9 = (f32[4,36,16,1]{1,2,3,0:T(8,128)}, f32[4,36,16,1]{1,2,3,0:T(8,128)S(1)}, u32[]{:S(2)}, u32[]{:S(2)}) collective-permute-start(f32[4,36,16,1]{1,2,3,0:T(8,128)} %copy.50), channel_id=1, source_target_pairs={{0,2},{1,3},{4,6},{5,7},{8,10},{9,11},{12,14},{13,15},{16,18},{17,... | collective-permute-start | bytes 27656 | tf_op jit(solution)/shard_map/ppermute | solution.py:30
  62.1 20.2 %copy-start.13 = (f32[768,8]{0,1:T(8,128)S(1)}, f32[768,8]{0,1:T(8,128)}, u32[]{:S(2)}) copy-start(f32[768,8]{0,1:T(8,128)} %param.17) | copy-start | bytes 73732
  62.1 21.2 %copy-start.14 = (pred[768,8]{0,1:T(8,128)(4,1)S(1)}, pred[768,8]{0,1:T(8,128)(4,1)}, u32[]{:S(2)}) copy-start(pred[768,8]{0,1:T(8,128)(4,1)} %get-tuple-element.8) | copy-start | bytes 18436
  66.9 5.5 %collective-permute-start.11 = (f32[4,16,128]{2,1,0:T(8,128)S(1)}, f32[4,16,128]{2,1,0:T(8,128)S(1)}, u32[]{:S(2)}, u32[]{:S(2)}) collective-permute-start(f32[4,16,128]{2,1,0:T(8,128)S(1)} %bitcast.38), channel_id=1, source_target_pairs={{4,0},{8,4},{12,8},{0,12},{5,1},{9,5},{13,9},{1,13},{6,2},{10,6},{... | collective-permute-start | bytes 98312 | tf_op jit(solution)/shard_map/ppermute | solution.py:32
  70.8 5.7 %collective-permute-start.10 = (f32[4,16,128]{2,1,0:T(8,128)S(1)}, f32[4,16,128]{2,1,0:T(8,128)S(1)}, u32[]{:S(2)}, u32[]{:S(2)}) collective-permute-start(f32[4,16,128]{2,1,0:T(8,128)S(1)} %bitcast.39), channel_id=1, source_target_pairs={{0,4},{4,8},{8,12},{12,0},{1,5},{5,9},{9,13},{13,1},{2,6},{6,10},{... | collective-permute-start | bytes 98312 | tf_op jit(solution)/shard_map/ppermute | solution.py:30
  76.5 8.2 %collective-permute-start.13 = (f32[4,48,128]{2,1,0:T(8,128)S(1)}, f32[4,48,128]{2,1,0:T(8,128)S(1)}, u32[]{:S(2)}, u32[]{:S(2)}) collective-permute-start(f32[4,48,128]{2,1,0:T(8,128)S(1)} %pad_maximum_fusion.1), channel_id=1, source_target_pairs={{2,0},{3,1},{6,4},{7,5},{10,8},{11,9},{14,12},{15,13},{18,16},{19,... | collective-permute-start | bytes 294920 | tf_op jit(solution)/shard_map/ppermute | solution.py:32
  77.8 7.0 %collective-permute-start.12 = (f32[4,48,128]{2,1,0:T(8,128)S(1)}, f32[4,48,128]{2,1,0:T(8,128)S(1)}, u32[]{:S(2)}, u32[]{:S(2)}) collective-permute-start(f32[4,48,128]{2,1,0:T(8,128)S(1)} %pad_maximum_fusion.1), channel_id=1, source_target_pairs={{0,2},{1,3},{4,6},{5,7},{8,10},{9,11},{12,14},{13,15},{16,18},{17,... | collective-permute-start | bytes 294920 | tf_op jit(solution)/shard_map/ppermute | solution.py:30
where the time goes:
time: 119 us; the launch traced here: 118 us
  local copies, waits for them, and re-layouts  57.2 us (48%)
  starting transfers between devices  31.8 us (27%)
  other arithmetic  13.7 us (12%)
  matrix products  8.44 us (7%)
  waiting for transfers between devices  5.98 us (5%)
    gather x1, local copies, waits for them, and re-layouts, body(): jnp.take(flat_surface, local_index.reshape(-1), axis=1)  19.8 us
    ppermute x6, starting transfers between devices, extended(): lax.ppermute(head, axis, [((i + 1) % count, i) for i in range(ends)])  16.6 us
    ppermute x6, starting transfers between devices, extended(): lax.ppermute(tail, axis, [(i, (i + 1) % count) for i in range(ends)])  13.9 us
    dot_general x2, matrix products, convect(): jnp.einsum('lk,alxy->akxy', matrix, adjoint, precision=lax.Precision.HIGH...  8.44 us
    unnamed x36, local copies, waits for them, and re-layouts  6.99 us
    reduce_sum x1, other arithmetic, body(): sensed = jnp.sum(margin_weight[None] * values, axis=2)  6.14 us
    reshape x1, local copies, waits for them, and re-layouts, body(): flat_surface = rim_cells.reshape(per_device, 9 * width_x * width_y)  5.69 us
    sub x1, other arithmetic, combine(): center * rate_sum + east_rate * east - west_rate * west + north_rate * north  4.72 us
  transfers between devices with their start and end apart: 14, of which 3 were waited for; matrix products, arithmetic and copies ran while one was open for 20% of the time, Pallas kernels for 0%

commit v1 on v0

v1 whole, which is shorter than its diff:
```python
import functools

import jax
import jax.numpy as jnp
from jax import lax
from jax.experimental import pallas as pl
from jax.experimental.pallas import tpu as pltpu
from jax.sharding import PartitionSpec as P

ADJ = 8
NSTEP = 2
MESH = pl.DeviceIdType.MESH


def offsets(count):
    return [0, 1, -1][: min(3, count)]


def slot_of(offset, count):
    return offset % min(3, count)


def divmod_const(value, number):
    if number & (number - 1) == 0:
        return value >> (number.bit_length() - 1), value & (number - 1)
    return value // number, value % number


def split(value):
    high = value.astype(jnp.bfloat16).astype(jnp.float32)
    return high, value - high


def stacked(value, depth):
    high, low = split(value)
    rows, lanes = value.shape
    parts = [high, low, high]
    if depth > 3 * rows:
        parts.append(jnp.zeros((depth - 3 * rows, lanes), jnp.float32))
    return jnp.concatenate(parts, axis=0).astype(jnp.bfloat16)


def kernel_body(
    dims,
    innovation,
    cluster,
    kernel,
    wind_x,
    wind_y,
    strength,
    matrix,
    cells,
    weights,
    field,
    sensed,
    base,
    face_x,
    south_rates,
    pack_a,
    pack_b,
    state,
    table,
    square,
    send_sem,
    recv_sem,
):
    levels, width, adjoints, n_t, n_s = dims
    padded = base.shape[1]
    lanes = base.shape[2]
    depth = square.shape[0]
    me_g = lax.axis_index("groups")
    me_t = lax.axis_index("tiles")
    me_s = lax.axis_index("sub")
    me_a = lax.axis_index("adj")
    nx, ny = min(3, n_t), min(3, n_s)

    def device(dt, ds):
        return (me_g, lax.rem(me_t + dt + n_t, n_t), lax.rem(me_s + ds + n_s, n_s), me_a)

    partners = [(dt, ds) for dt in offsets(n_t) for ds in offsets(n_s) if (dt, ds) != (0, 0)]
    barrier = pltpu.get_barrier_semaphore()
    for dt, ds in partners:
        pl.semaphore_signal(barrier, inc=1, device_id=device(dt, ds), device_id_type=MESH)

    count = [0]

    def send(src, dst, dt, ds):
        at = count[0]
        count[0] += 1
        copy = pltpu.make_async_remote_copy(
            src_ref=src,
            dst_ref=dst,
            send_sem=send_sem.at[at],
            recv_sem=recv_sem.at[at],
            device_id=device(dt, ds),
            device_id_type=MESH,
        )
        copy.start()
        return copy

    square[...] = jnp.zeros_like(square)
    square[0:levels, 0:levels] = matrix[...]
    high, low = split(square[...].T)
    mixer = high + pltpu.roll(high, padded, 1) + pltpu.roll(low, 2 * padded, 1)
    mixer = mixer[0:padded].astype(jnp.bfloat16)

    def mix(value):
        return jnp.dot(mixer, stacked(value, depth), preferred_element_type=jnp.float32)

    lane = lax.broadcasted_iota(jnp.int32, (padded, lanes), 1)
    pair = ((lane + 1) & (lanes - 1)) >> 1
    level = lax.broadcasted_iota(jnp.int32, (padded, lanes), 0)

    last = padded - 8

    def prepare(x, packed):
        rows = pl.ds(x, levels, stride=width)
        empty = jnp.zeros((8, lanes), jnp.float32)
        face_x[1 + x, last:padded, :] = empty
        south_rates[x, last:padded, :] = empty
        base[1 + x, last:padded, :] = empty
        face_x[1 + x, 0:levels, :] = wind_x[rows, :]
        south_rates[x, 0:levels, :] = wind_y[rows, :]
        base[1 + x, 0:levels, :] = kernel[rows, :]
        column = base[1 + x]
        one = pl.ds(x, 1)
        mixed = mix(column)
        column = (column + strength[one, :] * (mixed - column)) * innovation[one, :]
        column = jnp.where(level == levels, cluster[one, :].astype(jnp.float32), column)
        base[1 + x] = column
        packed = jnp.where(pair == x, pltpu.roll(column, 2 * x, 1), packed)
        faces = south_rates[x]
        packed = jnp.where(pair == width + x, pltpu.roll(faces, 2 * (width + x), 1), packed)
        return packed

    packed = jnp.zeros((padded, lanes), jnp.float32)
    packed = lax.fori_loop(0, width, prepare, packed)
    pack_a[0] = packed

    pl.semaphore_wait(barrier, len(partners))

    def send_pack(pack):
        return [
            send(pack.at[0], pack.at[slot_of(-ds, n_s)], 0, ds) for ds in offsets(n_s) if ds != 0
        ]

    copies = send_pack(pack_a)
    copies.append(send(base.at[1], base.at[width + 1], -1, 0))
    copies.append(send(base.at[width], base.at[0], 1, 0))
    copies.append(send(face_x.at[width], face_x.at[0], 1, 0))
    for copy in copies:
        copy.wait()

    odd = (lane & 1) == 1
    has_south = jnp.where(me_s > 0, 1.0, 0.0)
    has_north = jnp.where(me_s < n_s - 1, 1.0, 0.0)

    def merged(pack):
        south = pltpu.roll(pack[slot_of(-1, n_s)], 2, 1) * has_south
        north = pack[slot_of(1, n_s)] * has_north
        return jnp.where(odd, south, north)

    def edges(pack, at, value):
        seam = pltpu.roll(pack, lanes - 1 - 2 * at, 1)
        rows = lane[0 : value.shape[0]]
        north = jnp.where(rows == lanes - 1, seam, pltpu.roll(value, lanes - 1, 1))
        south = jnp.where(rows == 0, seam, pltpu.roll(value, 1, 1))
        return north, south

    seam_a = merged(pack_a)
    first_id = (me_a * adjoints).astype(jnp.float32)

    def advance(x, packed):
        face_y = south_rates[x]
        _, face_south = edges(seam_a, width + x, face_y)
        east_rate = jnp.maximum(face_x[1 + x], 0.0)
        west_rate = jnp.minimum(face_x[x], 0.0)
        north_rate = jnp.maximum(face_y, 0.0)
        south_rate = jnp.minimum(face_south, 0.0)
        center_rate = 1.0 - east_rate + west_rate - north_rate + south_rate
        center, east, west = base[1 + x], base[2 + x], base[x]
        north, south = edges(seam_a, x, center)
        terms = [
            (center * center_rate, center),
            (east * east_rate, east),
            (-west * west_rate, west),
            (north * north_rate, north),
            (-south * south_rate, south),
        ]
        values = []
        for a in range(adjoints):
            total = None
            for product, source in terms:
                ids = source[levels : levels + 1, :]
                chosen = jnp.where(ids == first_id + a, 1.0, 0.0)
                part = product * chosen
                total = part if total is None else total + part
            values.append(total)
        together = jnp.concatenate(values, axis=1)
        mixed = mix(together)
        fraction = strength[pl.ds(x, 1), :]
        for a in range(adjoints):
            value = values[a]
            value = value + fraction * (mixed[:, a * lanes : (a + 1) * lanes] - value)
            state[1 + x, a] = value
            at = a * width + x
            packed = jnp.where(pair == at, pltpu.roll(value, 2 * at, 1), packed)
        return packed

    packed = jnp.zeros((padded, lanes), jnp.float32)
    packed = advance(0, packed)
    packed = advance(width - 1, packed)
    copies = [
        send(state.at[1], state.at[width + 1], -1, 0),
        send(state.at[width], state.at[0], 1, 0),
    ]
    packed = lax.fori_loop(1, width - 1, advance, packed)
    pack_b[0] = packed
    copies += send_pack(pack_b)
    for copy in copies:
        copy.wait()
    seam_b = merged(pack_b)

    def transport(x, low, high):
        face_y = south_rates[x, low:high]
        _, face_south = edges(seam_a[low:high], width + x, face_y)
        east_rate = jnp.maximum(face_x[1 + x, low:high], 0.0)
        west_rate = jnp.minimum(face_x[x, low:high], 0.0)
        north_rate = jnp.maximum(face_y, 0.0)
        south_rate = jnp.minimum(face_south, 0.0)
        center_rate = 1.0 - east_rate + west_rate - north_rate + south_rate
        results = []
        for a in range(adjoints):
            center = state[1 + x, a, low:high]
            north, south = edges(seam_b[low:high], a * width + x, center)
            results.append(
                center * center_rate
                + east_rate * state[2 + x, a, low:high]
                - west_rate * state[x, a, low:high]
                + north_rate * north
                - south_rate * south
            )
        return results

    first = 8

    def surface(x, carry):
        for a, value in enumerate(transport(x, 0, first)):
            field[pl.ds(a * levels * width + x, first, stride=width), :] = value
            table[0, pl.ds(a * width + x, 1), :] = value[0:1, :]
        return carry

    lax.fori_loop(0, width, surface, 0)
    copies = []
    for dt, ds in partners:
        slot = slot_of(dt, n_t) * ny + slot_of(ds, n_s)
        there = slot_of(-dt, n_t) * ny + slot_of(-ds, n_s)
        copies.append(send(table.at[0], table.at[there], dt, ds))

    def rest(x, carry):
        for a, value in enumerate(transport(x, first, padded)):
            rows = pl.ds((a * levels + first) * width + x, levels - first, stride=width)
            field[rows, :] = value[0 : levels - first, :]
        return carry

    lax.fori_loop(0, width, rest, 0)

    column, row = divmod_const(cells[...], n_s * lanes)
    tile, in_tile = divmod_const(column, width)
    block, in_block = divmod_const(row, lanes)
    step_t = tile - me_t
    step_t = jnp.where(step_t < 0, step_t + n_t, step_t)
    step_t = jnp.where(step_t > 1, 2, step_t)
    step_s = block - me_s
    step_s = jnp.where(step_s < 0, step_s + ny, step_s)
    table_row = (step_t * ny + step_s) * width + in_tile
    elements = cells.shape[1]
    chunks = elements // lanes
    slots = cells.shape[0]

    for copy in copies:
        copy.wait()

    def pick(at, carry):
        slot, x = divmod_const(at, width)
        taken = list(carry)
        masks = [table_row[:, c * lanes : (c + 1) * lanes] == at for c in range(chunks)]
        for a in range(adjoints):
            line = jnp.broadcast_to(table[slot, pl.ds(a * width + x, 1), :], (slots, lanes))
            for c in range(chunks):
                found = jnp.take_along_axis(
                    line, in_block[:, c * lanes : (c + 1) * lanes], axis=1, mode="promise_in_bounds"
                )
                i = a * chunks + c
                taken[i] = jnp.where(masks[c], found, taken[i])
        return tuple(taken)

    empty = jnp.zeros((slots, lanes), jnp.float32)
    taken = lax.fori_loop(0, nx * ny * width, pick, (empty,) * (adjoints * chunks))
    for a in range(adjoints):
        for c in range(chunks):
            part = taken[a * chunks + c] * weights[:, c * lanes : (c + 1) * lanes]
            sensed[a : a + 1, c * lanes : (c + 1) * lanes] = jnp.sum(part, axis=0, keepdims=True)


def body(
    innovation,
    cluster,
    kernel,
    wind_x,
    wind_y,
    conv_strength,
    conv_matrix,
    margin_cell,
    margin_weight,
):
    levels, width, lanes = kernel.shape
    n_t, n_s = lax.axis_size("tiles"), lax.axis_size("sub")
    adjoints = ADJ // lax.axis_size("adj")
    elements, slots = margin_cell.shape
    padded = 8 * (levels // 8 + 1)
    depth = 128 * pl.cdiv(3 * padded, 128)
    nx, ny = min(3, n_t), min(3, n_s)
    n_sems = 2 * (ny - 1) + 5 + nx * ny - 1
    vmem = pl.BlockSpec(memory_space=pltpu.VMEM)
    field, sensed = pl.pallas_call(
        functools.partial(kernel_body, (levels, width, adjoints, n_t, n_s)),
        out_shape=(
            jax.ShapeDtypeStruct((adjoints * levels * width, lanes), jnp.float32),
            jax.ShapeDtypeStruct((adjoints, elements), jnp.float32),
        ),
        in_specs=[vmem] * 9,
        out_specs=(vmem, vmem),
        scratch_shapes=[
            pltpu.VMEM((width + 2, padded, lanes), jnp.float32),
            pltpu.VMEM((width + 2, padded, lanes), jnp.float32),
            pltpu.VMEM((width, padded, lanes), jnp.float32),
            pltpu.VMEM((ny, padded, lanes), jnp.float32),
            pltpu.VMEM((ny, padded, lanes), jnp.float32),
            pltpu.VMEM((width + 2, adjoints, padded, lanes), jnp.float32),
            pltpu.VMEM((nx * ny, adjoints * width, lanes), jnp.float32),
            pltpu.VMEM((depth, depth), jnp.float32),
            pltpu.SemaphoreType.DMA((n_sems,)),
            pltpu.SemaphoreType.DMA((n_sems,)),
        ],
        compiler_params=pltpu.CompilerParams(
            collective_id=0, has_side_effects=True, vmem_limit_bytes=48 * 1024 * 1024
        ),
    )(
        innovation,
        cluster,
        kernel.reshape(levels * width, lanes),
        wind_x.reshape(levels * width, lanes),
        wind_y.reshape(levels * width, lanes),
        conv_strength,
        conv_matrix,
        margin_cell.T,
        margin_weight.T,
    )
    return field.reshape(adjoints, levels, width, lanes), sensed


def solution(mesh):
    in_specs = (
        P(("groups", "tiles"), "sub"),
        P(("groups", "tiles"), "sub"),
        P(None, "tiles", "sub"),
        P(None, "tiles", "sub"),
        P(None, "tiles", "sub"),
        P("tiles", "sub"),
        P(),
        P(("tiles", "sub"), None),
        P(("tiles", "sub"), None),
    )
    out_specs = (P(("groups", "adj"), None, "tiles", "sub"), P(("groups", "adj"), ("tiles", "sub")))
    return jax.shard_map(body, mesh=mesh, in_specs=in_specs, out_specs=out_specs, check_vma=False)
```

time: 119 us -> 47.1 us (0.40)
  local copies, waits for them, and re-layouts: 57.2 us -> 8.78 us
  Pallas kernels: 0 us -> 37.1 us
  starting transfers between devices: 31.8 us -> 0 us
  other arithmetic: 13.7 us -> 0 us
  matrix products: 8.44 us -> 0 us
  waiting for transfers between devices: 5.98 us -> 0 us
    pallas_call x0 -> x1, Pallas kernels: none -> 37.1 us  [body(): pl.pallas_call(functools.partial(kernel_body, (levels, width, adjoints, n...]
    ppermute x14 -> x0, starting transfers between devices: 31.8 us -> none  [the longest x6 16.6 us: extended(): lax.ppermute(head, axis, [((i + 1) % count, i) for i in range(ends)])]
    gather x1 -> x0, local copies, waits for them, and re-layouts: 19.8 us -> none  [body(): jnp.take(flat_surface, local_index.reshape(-1), axis=1)]
    slice x15 -> x0, local copies, waits for them, and re-layouts: 17 us -> none  [the longest x4 4.67 us: body(): adjoint[:, :, :, -1:]]
    dot_general x2 -> x0, matrix products: 8.44 us -> none  [convect(): jnp.einsum('lk,alxy->akxy', matrix, adjoint, precision=lax.Precision.HIGH...]
    ppermute x4 -> x0, local copies, waits for them, and re-layouts: 6.63 us -> none  [the longest x2 3.35 us: extended(): lax.ppermute(tail, axis, [(i, (i + 1) % count) for i in range(ends)])]
    reduce_sum x1 -> x0, other arithmetic: 6.14 us -> none  [body(): sensed = jnp.sum(margin_weight[None] * values, axis=2)]
    ppermute x14 -> x0, waiting for transfers between devices: 5.98 us -> none  [the longest x6 4.4 us: extended(): lax.ppermute(tail, axis, [(i, (i + 1) % count) for i in range(ends)])]
  transfers between devices with their start and end apart: 14 -> 0, of which waited for: 3 -> 0; matrix products, arithmetic and copies ran while one was open for 20% -> 0% of each run, Pallas kernels for 0% -> 0%
where the time goes in v1:
time: 47.1 us; the launch traced here: 46.5 us
  Pallas kernels  37.1 us (79%)
  local copies, waits for them, and re-layouts  8.78 us (19%)
  between operations  0.66 us (1%)
    pallas_call x1, Pallas kernels, body(): pl.pallas_call(functools.partial(kernel_body, (levels, width, adjoints, n...  37.1 us
    unnamed x20, local copies, waits for them, and re-layouts  8.78 us

profile of v1, /device:TPU:0, one launch (start us, length us, event | category | flops | bytes accessed | tf_op | source)
XLA Modules:
  0.0 46.5 jit_solution(4233310821004991900)
XLA Ops:
  0.6 0.0 copy-start
  0.6 1.0 %copy-done = f32[36,16,128]{2,1,0:T(8,128)S(1)} copy-done((f32[36,16,128]{2,1,0:T(8,128)S(1)}, f32[36,16,128]{2,1,0:T(8,128)}, u32[]{:S(2)}) %copy-start) | copy-done | bytes 294936
  1.6 0.0 copy-start.1
  1.6 1.0 %copy-done.1 = f32[36,16,128]{2,1,0:T(8,128)S(1)} copy-done((f32[36,16,128]{2,1,0:T(8,128)S(1)}, f32[36,16,128]{2,1,0:T(8,128)}, u32[]{:S(2)}) %copy-start.1) | copy-done | bytes 294936
  2.6 0.0 copy-start.2
  2.6 1.0 %copy-done.2 = f32[36,16,128]{2,1,0:T(8,128)S(1)} copy-done((f32[36,16,128]{2,1,0:T(8,128)S(1)}, f32[36,16,128]{2,1,0:T(8,128)}, u32[]{:S(2)}) %copy-start.2) | copy-done | bytes 294936
  3.5 0.0 copy-start.3
  3.5 0.7 %copy-done.3 = s32[768,8]{0,1:T(8,128)S(1)} copy-done((s32[768,8]{0,1:T(8,128)S(1)}, s32[768,8]{0,1:T(8,128)}, u32[]{:S(2)}) %copy-start.3) | copy-done | bytes 24600
  4.3 0.0 copy-start.4
  4.3 0.7 %copy-done.4 = f32[768,8]{0,1:T(8,128)S(1)} copy-done((f32[768,8]{0,1:T(8,128)S(1)}, f32[768,8]{0,1:T(8,128)}, u32[]{:S(2)}) %copy-start.4) | copy-done | bytes 24600
  5.0 0.0 copy-start.5
  5.0 0.7 %copy-done.5 = f32[36,36]{1,0:T(8,128)S(1)} copy-done((f32[36,36]{1,0:T(8,128)S(1)}, f32[36,36]{1,0:T(8,128)}, u32[]{:S(2)}) %copy-start.5) | copy-done | bytes 5208
  5.7 0.0 copy-start.6
  5.7 0.7 %copy-done.6 = f32[16,128]{1,0:T(8,128)S(1)} copy-done((f32[16,128]{1,0:T(8,128)S(1)}, f32[16,128]{1,0:T(8,128)}, u32[]{:S(2)}) %copy-start.6) | copy-done | bytes 8216
  6.4 0.0 copy-start.7
  6.4 0.7 %copy-done.7 = s32[16,128]{1,0:T(8,128)S(1)} copy-done((s32[16,128]{1,0:T(8,128)S(1)}, s32[16,128]{1,0:T(8,128)}, u32[]{:S(2)}) %copy-start.7) | copy-done | bytes 8216
  7.1 0.0 copy-start.8
  7.1 0.7 %copy-done.8 = f32[16,128]{1,0:T(8,128)S(1)} copy-done((f32[16,128]{1,0:T(8,128)S(1)}, f32[16,128]{1,0:T(8,128)}, u32[]{:S(2)}) %copy-start.8) | copy-done | bytes 8216
  7.8 37.1 %shard_map.104 = (f32[2304,128]{1,0:T(8,128)S(1)}, f32[4,768]{1,0:T(4,128)S(1)}) custom-call(f32[16,128]{1,0:T(8,128)S(1)} %copy-done.6, s32[16,128]{1,0:T(8,128)S(1)} %copy-done.7, f32[576,128]{1,0:T(8,128)S(1)} %bitcast.7, f32[576,128]{1,0:T(8,128)S(1)} %bitcast.8, f32[576,128]{1,0:T(8,128)S(1)} %bitcast.9, f32[16,128]{1,0:T(8,128)S(1)} %copy-done.8, ...), custom_call_target="tpu_custom_call" | custom-call | tf_op jit(solution)/shard_map/pallas_call | solution.py:326
  44.9 1.0 %copy.13 = f32[4,36,16,128]{3,2,1,0:T(8,128)} copy(f32[4,36,16,128]{3,2,1,0:T(8,128)S(1)} %bitcast.6) | data formatting | bytes 2359296
  45.9 0.6 %copy.14 = f32[4,768]{1,0:T(4,128)} copy(f32[4,768]{1,0:T(4,128)S(1)} %get-tuple-element.9) | data formatting | bytes 24576
Async XLA Ops:
  0.6 1.0 %copy-start = (f32[36,16,128]{2,1,0:T(8,128)S(1)}, f32[36,16,128]{2,1,0:T(8,128)}, u32[]{:S(2)}) copy-start(f32[36,16,128]{2,1,0:T(8,128)} %param.11) | copy-start | bytes 884740
  1.6 1.0 %copy-start.1 = (f32[36,16,128]{2,1,0:T(8,128)S(1)}, f32[36,16,128]{2,1,0:T(8,128)}, u32[]{:S(2)}) copy-start(f32[36,16,128]{2,1,0:T(8,128)} %param.12) | copy-start | bytes 884740
  2.6 1.0 %copy-start.2 = (f32[36,16,128]{2,1,0:T(8,128)S(1)}, f32[36,16,128]{2,1,0:T(8,128)}, u32[]{:S(2)}) copy-start(f32[36,16,128]{2,1,0:T(8,128)} %param.13) | copy-start | bytes 884740
  3.5 0.7 %copy-start.3 = (s32[768,8]{0,1:T(8,128)S(1)}, s32[768,8]{0,1:T(8,128)}, u32[]{:S(2)}) copy-start(s32[768,8]{0,1:T(8,128)} %param.16) | copy-start | bytes 73732
  4.3 0.7 %copy-start.4 = (f32[768,8]{0,1:T(8,128)S(1)}, f32[768,8]{0,1:T(8,128)}, u32[]{:S(2)}) copy-start(f32[768,8]{0,1:T(8,128)} %param.17) | copy-start | bytes 73732
  5.0 0.7 %copy-start.5 = (f32[36,36]{1,0:T(8,128)S(1)}, f32[36,36]{1,0:T(8,128)}, u32[]{:S(2)}) copy-start(f32[36,36]{1,0:T(8,128)} %matrix.1) | copy-start | bytes 15556
  5.7 0.7 %copy-start.6 = (f32[16,128]{1,0:T(8,128)S(1)}, f32[16,128]{1,0:T(8,128)}, u32[]{:S(2)}) copy-start(f32[16,128]{1,0:T(8,128)} %innovation.1) | copy-start | bytes 24580
  6.4 0.7 %copy-start.7 = (s32[16,128]{1,0:T(8,128)S(1)}, s32[16,128]{1,0:T(8,128)}, u32[]{:S(2)}) copy-start(s32[16,128]{1,0:T(8,128)} %cluster.1) | copy-start | bytes 24580
  7.1 0.7 %copy-start.8 = (f32[16,128]{1,0:T(8,128)S(1)}, f32[16,128]{1,0:T(8,128)}, u32[]{:S(2)}) copy-start(f32[16,128]{1,0:T(8,128)} %strength.1) | copy-start | bytes 24580

commit v2 on v1

--- a/solution.py
+++ b/solution.py
@@ -42,28 +42,24 @@
 
 def kernel_body(
     dims,
-    innovation,
-    cluster,
-    kernel,
-    wind_x,
-    wind_y,
-    strength,
-    matrix,
-    cells,
-    weights,
-    field,
-    sensed,
-    base,
-    face_x,
-    south_rates,
-    pack_a,
-    pack_b,
-    state,
-    table,
-    square,
-    send_sem,
-    recv_sem,
+    *refs,
 ):
+    sources, (field, sensed), scratch = refs[:9], refs[9:11], refs[11:]
+    arrivals, scratch = scratch[:9], scratch[9:]
+    innovation, cluster, kernel, wind_x, wind_y, strength, matrix, cells, weights = arrivals
+    (
+        base,
+        face_x,
+        south_rates,
+        pack_a,
+        pack_b,
+        state,
+        table,
+        square,
+        send_sem,
+        recv_sem,
+        load_sem,
+    ) = scratch
     levels, width, adjoints, n_t, n_s = dims
     padded = base.shape[1]
     lanes = base.shape[2]
@@ -81,6 +77,12 @@
     barrier = pltpu.get_barrier_semaphore()
     for dt, ds in partners:
         pl.semaphore_signal(barrier, inc=1, device_id=device(dt, ds), device_id_type=MESH)
+    loads = [
+        pltpu.make_async_copy(source, arrival, load_sem.at[i])
+        for i, (source, arrival) in enumerate(zip(sources, arrivals))
+    ]
+    for i in (6, 2, 0, 1, 5, 3, 4, 7, 8):
+        loads[i].start()
 
     count = [0]
 
@@ -99,6 +101,7 @@
         return copy
 
     square[...] = jnp.zeros_like(square)
+    loads[6].wait()
     square[0:levels, 0:levels] = matrix[...]
     high, low = split(square[...].T)
     mixer = high + pltpu.roll(high, padded, 1) + pltpu.roll(low, 2 * padded, 1)
@@ -112,6 +115,9 @@
     level = lax.broadcasted_iota(jnp.int32, (padded, lanes), 0)
 
     last = padded - 8
+
+    for load in loads[:6]:
+        load.wait()
 
     def prepare(x, packed):
         rows = pl.ds(x, levels, stride=width)
@@ -133,21 +139,23 @@
         packed = jnp.where(pair == width + x, pltpu.roll(faces, 2 * (width + x), 1), packed)
         return packed
 
-    packed = jnp.zeros((padded, lanes), jnp.float32)
-    packed = lax.fori_loop(0, width, prepare, packed)
-    pack_a[0] = packed
-
-    pl.semaphore_wait(barrier, len(partners))
-
     def send_pack(pack):
         return [
             send(pack.at[0], pack.at[slot_of(-ds, n_s)], 0, ds) for ds in offsets(n_s) if ds != 0
         ]
 
-    copies = send_pack(pack_a)
-    copies.append(send(base.at[1], base.at[width + 1], -1, 0))
-    copies.append(send(base.at[width], base.at[0], 1, 0))
-    copies.append(send(face_x.at[width], face_x.at[0], 1, 0))
+    packed = jnp.zeros((padded, lanes), jnp.float32)
+    packed = prepare(0, packed)
+    packed = prepare(width - 1, packed)
+    pl.semaphore_wait(barrier, len(partners))
+    copies = [
+        send(face_x.at[width], face_x.at[0], 1, 0),
+        send(base.at[width], base.at[0], 1, 0),
+        send(base.at[1], base.at[width + 1], -1, 0),
+    ]
+    packed = lax.fori_loop(1, width - 1, prepare, packed, unroll=True)
+    pack_a[0] = packed
+    copies += send_pack(pack_a)
     for copy in copies:
         copy.wait()
 
@@ -214,7 +222,7 @@
         send(state.at[1], state.at[width + 1], -1, 0),
         send(state.at[width], state.at[0], 1, 0),
     ]
-    packed = lax.fori_loop(1, width - 1, advance, packed)
+    packed = lax.fori_loop(1, width - 1, advance, packed, unroll=True)
     pack_b[0] = packed
     copies += send_pack(pack_b)
     for copy in copies:
@@ -250,7 +258,7 @@
             table[0, pl.ds(a * width + x, 1), :] = value[0:1, :]
         return carry
 
-    lax.fori_loop(0, width, surface, 0)
+    lax.fori_loop(0, width, surface, 0, unroll=True)
     copies = []
     for dt, ds in partners:
         slot = slot_of(dt, n_t) * ny + slot_of(ds, n_s)
@@ -263,8 +271,10 @@
             field[rows, :] = value[0 : levels - first, :]
         return carry
 
-    lax.fori_loop(0, width, rest, 0)
-
+    lax.fori_loop(0, width, rest, 0, unroll=True)
+
+    loads[7].wait()
+    loads[8].wait()
     column, row = divmod_const(cells[...], n_s * lanes)
     tile, in_tile = divmod_const(column, width)
     block, in_block = divmod_const(row, lanes)
@@ -296,7 +306,7 @@
         return tuple(taken)
 
     empty = jnp.zeros((slots, lanes), jnp.float32)
-    taken = lax.fori_loop(0, nx * ny * width, pick, (empty,) * (adjoints * chunks))
+    taken = lax.fori_loop(0, nx * ny * width, pick, (empty,) * (adjoints * chunks), unroll=4)
     for a in range(adjoints):
         for c in range(chunks):
             part = taken[a * chunks + c] * weights[:, c * lanes : (c + 1) * lanes]
@@ -323,15 +333,27 @@
     nx, ny = min(3, n_t), min(3, n_s)
     n_sems = 2 * (ny - 1) + 5 + nx * ny - 1
     vmem = pl.BlockSpec(memory_space=pltpu.VMEM)
+    operands = (
+        innovation,
+        cluster,
+        kernel.reshape(levels * width, lanes),
+        wind_x.reshape(levels * width, lanes),
+        wind_y.reshape(levels * width, lanes),
+        conv_strength,
+        conv_matrix,
+        margin_cell.T,
+        margin_weight.T,
+    )
     field, sensed = pl.pallas_call(
         functools.partial(kernel_body, (levels, width, adjoints, n_t, n_s)),
         out_shape=(
             jax.ShapeDtypeStruct((adjoints * levels * width, lanes), jnp.float32),
             jax.ShapeDtypeStruct((adjoints, elements), jnp.float32),
         ),
-        in_specs=[vmem] * 9,
+        in_specs=[pl.BlockSpec(memory_space=pltpu.HBM)] * 9,
         out_specs=(vmem, vmem),
-        scratch_shapes=[
+        scratch_shapes=[pltpu.VMEM(x.shape, x.dtype) for x in operands]
+        + [
             pltpu.VMEM((width + 2, padded, lanes), jnp.float32),
             pltpu.VMEM((width + 2, padded, lanes), jnp.float32),
             pltpu.VMEM((width, padded, lanes), jnp.float32),
@@ -342,21 +364,12 @@
             pltpu.VMEM((depth, depth), jnp.float32),
             pltpu.SemaphoreType.DMA((n_sems,)),
             pltpu.SemaphoreType.DMA((n_sems,)),
+            pltpu.SemaphoreType.DMA((len(operands),)),
         ],
         compiler_params=pltpu.CompilerParams(
-            collective_id=0, has_side_effects=True, vmem_limit_bytes=48 * 1024 * 1024
+            collective_id=0, has_side_effects=True, vmem_limit_bytes=60 * 1024 * 1024
         ),
-    )(
-        innovation,
-        cluster,
-        kernel.reshape(levels * width, lanes),
-        wind_x.reshape(levels * width, lanes),
-        wind_y.reshape(levels * width, lanes),
-        conv_strength,
-        conv_matrix,
-        margin_cell.T,
-        margin_weight.T,
-    )
+    )(*operands)
     return field.reshape(adjoints, levels, width, lanes), sensed
 
 

time: 47.1 us -> 32.6 us (0.69)
  Pallas kernels: 37.1 us -> 28.8 us
  local copies, waits for them, and re-layouts: 8.78 us -> 2.97 us
    pallas_call x1, Pallas kernels: 37.1 us -> 28.8 us  [body(): pl.pallas_call(functools.partial(kernel_body, (levels, width, adjoints, n...]
    unnamed x20 -> x4, local copies, waits for them, and re-layouts: 8.78 us -> 2.97 us
where the time goes in v2:
time: 32.6 us; the launch traced here: 32.4 us
  Pallas kernels  28.8 us (88%)
  local copies, waits for them, and re-layouts  2.97 us (9%)
  between operations  0.65 us (2%)
    pallas_call x1, Pallas kernels, body(): pl.pallas_call(functools.partial(kernel_body, (levels, width, adjoints, n...  28.8 us
    unnamed x4, local copies, waits for them, and re-layouts  2.97 us

profile of v2, /device:TPU:0, one launch (start us, length us, event | category | flops | bytes accessed | tf_op | source)
XLA Modules:
  0.0 32.4 jit_solution(6770476151369007825)
XLA Ops:
  0.6 28.8 %shard_map.104 = (f32[2304,128]{1,0:T(8,128)}, f32[4,768]{1,0:T(4,128)}) custom-call(f32[16,128]{1,0:T(8,128)} %refs_0_.1, s32[16,128]{1,0:T(8,128)} %refs_1_.1, f32[576,128]{1,0:T(8,128)} %bitcast.7, f32[576,128]{1,0:T(8,128)} %bitcast.8, f32[576,128]{1,0:T(8,128)} %bitcast.9, f32[16,128]{1,0:T(8,128)} %refs_5_.1, f32[36,36]{1,0:T(8,128)} %refs_6_.1, ...), custom_call_target="tpu_custom_call" | custom-call | tf_op jit(solution)/shard_map/pallas_call | solution.py:347
  29.4 0.0 copy-start
  29.4 2.4 %copy.13 = f32[4,36,16,128]{3,2,1,0:T(8,128)} copy(f32[4,36,16,128]{3,2,1,0:T(8,128)} %bitcast.6) | data formatting | bytes 2359296
  31.8 0.0 copy-done
  31.8 0.6 %copy.14 = f32[4,768]{1,0:T(4,128)} copy(f32[4,768]{1,0:T(4,128)S(1)} %copy-done) | data formatting | bytes 24576
Async XLA Ops:
  29.4 2.4 %copy-start = (f32[4,768]{1,0:T(4,128)S(1)}, f32[4,768]{1,0:T(4,128)}, u32[]{:S(2)}) copy-start(f32[4,768]{1,0:T(4,128)} %get-tuple-element.9) | copy-start | bytes 36868

commit v3 on v2

v3 whole, which is shorter than its diff:
```python
import functools

import jax
import jax.numpy as jnp
from jax import lax
from jax.experimental import pallas as pl
from jax.experimental.pallas import tpu as pltpu
from jax.sharding import PartitionSpec as P

ADJ = 8
NSTEP = 2
MESH = pl.DeviceIdType.MESH


def offsets(count):
    return [0, 1, -1][: min(3, count)]


def slot_of(offset, count):
    return offset % min(3, count)


def divmod_const(value, number):
    if number & (number - 1) == 0:
        return value >> (number.bit_length() - 1), value & (number - 1)
    return value // number, value % number


def split(value):
    high = value.astype(jnp.bfloat16).astype(jnp.float32)
    return high, value - high


def stacked(value, depth):
    high, low = split(value)
    rows, lanes = value.shape
    parts = [high, low, high]
    if depth > 3 * rows:
        parts.append(jnp.zeros((depth - 3 * rows, lanes), jnp.float32))
    return jnp.concatenate(parts, axis=0).astype(jnp.bfloat16)


def kernel_body(
    dims,
    *refs,
):
    sources, (field, surfaces), scratch = refs[:7], refs[7:9], refs[9:]
    arrivals, scratch = scratch[:7], scratch[7:]
    innovation, cluster, kernel, wind_x, wind_y, strength, matrix = arrivals
    (
        base,
        face_x,
        face_y,
        pack_a,
        pack_b,
        state,
        table,
        held,
        square,
        send_sem,
        recv_sem,
        load_sem,
        store_sem,
    ) = scratch
    levels, width, adjoints, n_t, n_s = dims
    padded = base.shape[1]
    lanes = base.shape[2]
    depth = square.shape[0]
    me_g = lax.axis_index("groups")
    me_t = lax.axis_index("tiles")
    me_s = lax.axis_index("sub")
    me_a = lax.axis_index("adj")
    nx, ny = min(3, n_t), min(3, n_s)

    def device(dt, ds):
        return (me_g, lax.rem(me_t + dt + n_t, n_t), lax.rem(me_s + ds + n_s, n_s), me_a)

    partners = [(dt, ds) for dt in offsets(n_t) for ds in offsets(n_s) if (dt, ds) != (0, 0)]
    barrier = pltpu.get_barrier_semaphore()
    for dt, ds in partners:
        pl.semaphore_signal(barrier, inc=1, device_id=device(dt, ds), device_id_type=MESH)
    loads = [
        pltpu.make_async_copy(source, arrival, load_sem.at[i])
        for i, (source, arrival) in enumerate(zip(sources, arrivals))
    ]
    for i in (6, 2, 0, 1, 5, 3, 4):
        loads[i].start()

    count = [0]

    def send(src, dst, dt, ds):
        at = count[0]
        count[0] += 1
        copy = pltpu.make_async_remote_copy(
            src_ref=src,
            dst_ref=dst,
            send_sem=send_sem.at[at],
            recv_sem=recv_sem.at[at],
            device_id=device(dt, ds),
            device_id_type=MESH,
        )
        copy.start()
        return copy

    square[...] = jnp.zeros_like(square)
    loads[6].wait()
    square[0:levels, 0:levels] = matrix[...]
    high, low = split(square[...].T)
    mixer = high + pltpu.roll(high, padded, 1) + pltpu.roll(low, 2 * padded, 1)
    mixer = mixer[0:padded].astype(jnp.bfloat16)

    def mix(value):
        return jnp.dot(mixer, stacked(value, depth), preferred_element_type=jnp.float32)

    lane = lax.broadcasted_iota(jnp.int32, (padded, lanes), 1)
    pair = ((lane + 1) & (lanes - 1)) >> 1
    level = lax.broadcasted_iota(jnp.int32, (padded, lanes), 0)

    last = levels // 8 * 8
    for load in loads[:6]:
        load.wait()

    def prepare(x, packed):
        rows = pl.ds(x, levels, stride=width)
        empty = jnp.zeros((padded - last, lanes), jnp.float32)
        face_x[2 + x, last:padded, :] = empty
        face_y[1 + x, last:padded, :] = empty
        base[2 + x, last:padded, :] = empty
        face_x[2 + x, 0:levels, :] = wind_x[rows, :]
        face_y[1 + x, 0:levels, :] = wind_y[rows, :]
        base[2 + x, 0:levels, :] = kernel[rows, :]
        column = base[2 + x]
        one = pl.ds(x, 1)
        mixed = mix(column)
        column = (column + strength[one, :] * (mixed - column)) * innovation[one, :]
        column = jnp.where(level == levels, cluster[one, :].astype(jnp.float32), column)
        column = jnp.where(level == levels + 1, strength[one, :], column)
        base[2 + x] = column
        packed = jnp.where(pair == x, pltpu.roll(column, 2 * x, 1), packed)
        faces = face_y[1 + x]
        packed = jnp.where(pair == width + x, pltpu.roll(faces, 2 * (width + x), 1), packed)
        return packed

    packed = jnp.zeros((padded, lanes), jnp.float32)
    for x in (0, 1, width - 2, width - 1):
        packed = prepare(x, packed)
    pl.semaphore_wait(barrier, len(partners))
    copies_x = [
        send(base.at[pl.ds(width, 2)], base.at[pl.ds(0, 2)], 1, 0),
        send(base.at[pl.ds(2, 2)], base.at[pl.ds(width + 2, 2)], -1, 0),
        send(face_x.at[pl.ds(width, 2)], face_x.at[pl.ds(0, 2)], 1, 0),
        send(face_x.at[2], face_x.at[width + 2], -1, 0),
        send(face_y.at[width], face_y.at[0], 1, 0),
        send(face_y.at[1], face_y.at[width + 1], -1, 0),
    ]
    packed = lax.fori_loop(2, width - 2, prepare, packed, unroll=True)
    pack_a[0] = packed
    near, far = [], []
    for dt, ds in partners:
        if ds != 0:
            there = slot_of(-dt, n_t) * ny + slot_of(-ds, n_s)
            copy = send(pack_a.at[0], pack_a.at[there], dt, ds)
            (far if dt else near).append(copy)
    for copy in near:
        copy.wait()

    odd = (lane & 1) == 1
    has_south = jnp.where(me_s > 0, 1.0, 0.0)
    has_north = jnp.where(me_s < n_s - 1, 1.0, 0.0)

    def merged(pack, dt):
        row = slot_of(dt, n_t) * ny
        south = pltpu.roll(pack[row + slot_of(-1, n_s)], 2, 1) * has_south
        north = pack[row + slot_of(1, n_s)] * has_north
        return jnp.where(odd, south, north)

    def edges(pack, at, value):
        seam = pltpu.roll(pack, lanes - 1 - 2 * at, 1)
        rows = lane[0 : value.shape[0]]
        north = jnp.where(rows == lanes - 1, seam, pltpu.roll(value, lanes - 1, 1))
        south = jnp.where(rows == 0, seam, pltpu.roll(value, 1, 1))
        return north, south

    seam_a = merged(pack_a, 0)
    first_id = (me_a * adjoints).astype(jnp.float32)

    def advance(x, seam, at):
        flow_y = face_y[1 + x]
        _, flow_south = edges(seam, width + at, flow_y)
        east_rate = jnp.maximum(face_x[2 + x], 0.0)
        west_rate = jnp.minimum(face_x[1 + x], 0.0)
        north_rate = jnp.maximum(flow_y, 0.0)
        south_rate = jnp.minimum(flow_south, 0.0)
        center_rate = 1.0 - east_rate + west_rate - north_rate + south_rate
        center, east, west = base[2 + x], base[3 + x], base[1 + x]
        north, south = edges(seam, at, center)
        terms = [
            (center * center_rate, center),
            (east * east_rate, east),
            (-west * west_rate, west),
            (north * north_rate, north),
            (-south * south_rate, south),
        ]
        values = []
        for a in range(adjoints):
            total = None
            for product, source in terms:
                ids = source[levels : levels + 1, :]
                chosen = jnp.where(ids == first_id + a, 1.0, 0.0)
                part = product * chosen
                total = part if total is None else total + part
            values.append(total)
        mixed = mix(jnp.concatenate(values, axis=1))
        fraction = center[levels + 1 : levels + 2, :]
        results = []
        for a in range(adjoints):
            value = values[a]
            value = value + fraction * (mixed[:, a * lanes : (a + 1) * lanes] - value)
            state[1 + x, a] = value
            results.append(value)
        return results

    def inside(x, packed):
        for a, value in enumerate(advance(x, seam_a, x)):
            at = a * width + x
            packed = jnp.where(pair == at, pltpu.roll(value, 2 * at, 1), packed)
        return packed

    packed = jnp.zeros((padded, lanes), jnp.float32)
    packed = lax.fori_loop(1, width - 1, inside, packed, unroll=True)
    for copy in copies_x:
        copy.wait()
    packed = inside(0, packed)
    packed = inside(width - 1, packed)
    pack_b[0] = packed
    copies = [
        send(pack_b.at[0], pack_b.at[slot_of(-ds, n_s)], 0, ds) for ds in offsets(n_s) if ds != 0
    ]
    for copy in far:
        copy.wait()
    advance(-1, merged(pack_a, -1), width - 1)
    advance(width, merged(pack_a, 1), 0)
    for copy in copies:
        copy.wait()
    seam_b = merged(pack_b, 0)

    stores = []

    def transport(low, high):
        top = min(high, levels)

        def along(x, carry):
            flow_y = face_y[1 + x, low:high]
            _, flow_south = edges(seam_a[low:high], width + x, flow_y)
            east_rate = jnp.maximum(face_x[2 + x, low:high], 0.0)
            west_rate = jnp.minimum(face_x[1 + x, low:high], 0.0)
            north_rate = jnp.maximum(flow_y, 0.0)
            south_rate = jnp.minimum(flow_south, 0.0)
            center_rate = 1.0 - east_rate + west_rate - north_rate + south_rate
            for a in range(adjoints):
                center = state[1 + x, a, low:high]
                north, south = edges(seam_b[low:high], a * width + x, center)
                value = (
                    center * center_rate
                    + east_rate * state[2 + x, a, low:high]
                    - west_rate * state[x, a, low:high]
                    + north_rate * north
                    - south_rate * south
                )
                rows = pl.ds((a * levels + low) * width + x, top - low, stride=width)
                held[rows, :] = value[0 : top - low, :]
                if low == 0:
                    table[0, pl.ds(a * width + x, 1), :] = value[0:1, :]
            return carry

        lax.fori_loop(0, width, along, 0, unroll=True)

    def store(low, high):
        top = min(high, levels)
        for a in range(adjoints):
            rows = pl.ds((a * levels + low) * width, (top - low) * width)
            copy = pltpu.make_async_copy(held.at[rows], field.at[rows], store_sem.at[len(stores)])
            copy.start()
            stores.append(copy)

    transport(0, 8)
    copies = []
    for dt, ds in partners:
        there = slot_of(-dt, n_t) * ny + slot_of(-ds, n_s)
        copies.append(send(table.at[0], table.at[there], dt, ds))
    store(0, 8)
    for low in range(8, padded, 8):
        transport(low, low + 8)
        store(low, low + 8)
    for copy in copies:
        copy.wait()
    own = pltpu.make_async_copy(table, surfaces, store_sem.at[len(stores)])
    own.start()
    for copy in stores:
        copy.wait()
    own.wait()


def gather_body(dims, cells, weights, surfaces, field, field_out, sensed, table, copy_sem, table_sem):
    width, adjoints, n_t, n_s = dims
    lanes = table.shape[2]
    nx, ny = min(3, n_t), min(3, n_s)
    me_t = lax.axis_index("tiles")
    me_s = lax.axis_index("sub")
    arrival = pltpu.make_async_copy(surfaces, table, table_sem)
    arrival.start()
    share = field.shape[0] // adjoints
    copies = []
    for a in range(adjoints):
        rows = pl.ds(a * share, share)
        copy = pltpu.make_async_copy(field.at[rows], field_out.at[rows], copy_sem.at[a])
        copy.start()
        copies.append(copy)

    column, row = divmod_const(cells[...], n_s * lanes)
    tile, in_tile = divmod_const(column, width)
    block, in_block = divmod_const(row, lanes)
    step_t = tile - me_t
    step_t = jnp.where(step_t < 0, step_t + n_t, step_t)
    step_t = jnp.where(step_t > 1, 2, step_t)
    step_s = block - me_s
    step_s = jnp.where(step_s < 0, step_s + ny, step_s)
    table_row = (step_t * ny + step_s) * width + in_tile
    elements = cells.shape[1]
    chunks = elements // lanes
    slots = cells.shape[0]

    arrival.wait()

    def pick(at, carry):
        slot, x = divmod_const(at, width)
        taken = list(carry)
        masks = [table_row[:, c * lanes : (c + 1) * lanes] == at for c in range(chunks)]
        for a in range(adjoints):
            line = jnp.broadcast_to(table[slot, pl.ds(a * width + x, 1), :], (slots, lanes))
            for c in range(chunks):
                found = jnp.take_along_axis(
                    line, in_block[:, c * lanes : (c + 1) * lanes], axis=1, mode="promise_in_bounds"
                )
                i = a * chunks + c
                taken[i] = jnp.where(masks[c], found, taken[i])
        return tuple(taken)

    empty = jnp.zeros((slots, lanes), jnp.float32)
    taken = lax.fori_loop(0, nx * ny * width, pick, (empty,) * (adjoints * chunks), unroll=4)
    for a in range(adjoints):
        for c in range(chunks):
            part = taken[a * chunks + c] * weights[:, c * lanes : (c + 1) * lanes]
            sensed[a : a + 1, c * lanes : (c + 1) * lanes] = jnp.sum(part, axis=0, keepdims=True)
    for copy in copies:
        copy.wait()


def body(
    innovation,
    cluster,
    kernel,
    wind_x,
    wind_y,
    conv_strength,
    conv_matrix,
    margin_cell,
    margin_weight,
):
    levels, width, lanes = kernel.shape
    n_t, n_s = lax.axis_size("tiles"), lax.axis_size("sub")
    adjoints = ADJ // lax.axis_size("adj")
    elements, slots = margin_cell.shape
    padded = 8 * pl.cdiv(levels + 2, 8)
    depth = 128 * pl.cdiv(3 * padded, 128)
    nx, ny = min(3, n_t), min(3, n_s)
    n_sems = 6 + 2 * (nx * ny - 1) - (nx - 1) + ny - 1
    anywhere = pl.BlockSpec(memory_space=pl.ANY)
    vmem = pl.BlockSpec(memory_space=pltpu.VMEM)
    limit = 60 * 1024 * 1024
    operands = (
        innovation,
        cluster,
        kernel.reshape(levels * width, lanes),
        wind_x.reshape(levels * width, lanes),
        wind_y.reshape(levels * width, lanes),
        conv_strength,
        conv_matrix,
    )
    field_shape = jax.ShapeDtypeStruct((adjoints * levels * width, lanes), jnp.float32)
    table_shape = jax.ShapeDtypeStruct((nx * ny, adjoints * width, lanes), jnp.float32)
    field, surfaces = pl.pallas_call(
        functools.partial(kernel_body, (levels, width, adjoints, n_t, n_s)),
        out_shape=(field_shape, table_shape),
        in_specs=[anywhere] * len(operands),
        out_specs=(anywhere, anywhere),
        scratch_shapes=[pltpu.VMEM(x.shape, x.dtype) for x in operands]
        + [
            pltpu.VMEM((width + 4, padded, lanes), jnp.float32),
            pltpu.VMEM((width + 3, padded, lanes), jnp.float32),
            pltpu.VMEM((width + 2, padded, lanes), jnp.float32),
            pltpu.VMEM((nx * ny, padded, lanes), jnp.float32),
            pltpu.VMEM((ny, padded, lanes), jnp.float32),
            pltpu.VMEM((width + 2, adjoints, padded, lanes), jnp.float32),
            pltpu.VMEM(table_shape.shape, jnp.float32),
            pltpu.VMEM(field_shape.shape, jnp.float32),
            pltpu.VMEM((depth, depth), jnp.float32),
            pltpu.SemaphoreType.DMA((n_sems,)),
            pltpu.SemaphoreType.DMA((n_sems,)),
            pltpu.SemaphoreType.DMA((len(operands),)),
            pltpu.SemaphoreType.DMA((adjoints * padded // 8 + 1,)),
        ],
        compiler_params=pltpu.CompilerParams(
            collective_id=0, has_side_effects=True, vmem_limit_bytes=limit
        ),
    )(*operands)
    field, sensed = pl.pallas_call(
        functools.partial(gather_body, (width, adjoints, n_t, n_s)),
        out_shape=(field_shape, jax.ShapeDtypeStruct((adjoints, elements), jnp.float32)),
        in_specs=[vmem, vmem, anywhere, anywhere],
        out_specs=(anywhere, vmem),
        scratch_shapes=[
            pltpu.VMEM(table_shape.shape, jnp.float32),
            pltpu.SemaphoreType.DMA((adjoints,)),
            pltpu.SemaphoreType.DMA,
        ],
        compiler_params=pltpu.CompilerParams(vmem_limit_bytes=limit),
    )(margin_cell.T, margin_weight.T, surfaces, field)
    return field.reshape(adjoints, levels, width, lanes), sensed


def solution(mesh):
    in_specs = (
        P(("groups", "tiles"), "sub"),
        P(("groups", "tiles"), "sub"),
        P(None, "tiles", "sub"),
        P(None, "tiles", "sub"),
        P(None, "tiles", "sub"),
        P("tiles", "sub"),
        P(),
        P(("tiles", "sub"), None),
        P(("tiles", "sub"), None),
    )
    out_specs = (P(("groups", "adj"), None, "tiles", "sub"), P(("groups", "adj"), ("tiles", "sub")))
    return jax.shard_map(body, mesh=mesh, in_specs=in_specs, out_specs=out_specs, check_vma=False)
```

time: 32.6 us -> 61.4 us (1.88)
  Pallas kernels: 28.8 us -> 60.5 us
  local copies, waits for them, and re-layouts: 2.97 us -> 0 us
    pallas_call x0 -> x1, Pallas kernels: none -> 38.2 us  [body(): pl.pallas_call(functools.partial(gather_body, (width, adjoints, n_t, n_s)...]
    pallas_call x1, Pallas kernels: 28.8 us -> 22.3 us  [body(): pl.pallas_call(functools.partial(kernel_body, (levels, width, adjoints, n...]
    unnamed x4 -> x0, local copies, waits for them, and re-layouts: 2.97 us -> none
where the time goes in v3:
time: 61.4 us; the launch traced here: 61.1 us
  Pallas kernels  60.5 us (99%)
  between operations  0.64 us (1%)
    pallas_call x1, Pallas kernels, body(): pl.pallas_call(functools.partial(gather_body, (width, adjoints, n_t, n_s)...  38.2 us
    pallas_call x1, Pallas kernels, body(): pl.pallas_call(functools.partial(kernel_body, (levels, width, adjoints, n...  22.3 us

profile of v3, /device:TPU:0, one launch (start us, length us, event | category | flops | bytes accessed | tf_op | source)
XLA Modules:
  0.0 61.1 jit_solution(13233719991776617718)
XLA Ops:
  0.6 22.3 %shard_map.104 = (f32[2304,128]{1,0:T(8,128)}, f32[6,64,128]{2,1,0:T(8,128)}) custom-call(f32[16,128]{1,0:T(8,128)} %refs_0_.1, s32[16,128]{1,0:T(8,128)} %refs_1_.1, f32[576,128]{1,0:T(8,128)} %bitcast.6, f32[576,128]{1,0:T(8,128)} %bitcast.7, f32[576,128]{1,0:T(8,128)} %bitcast.8, f32[16,128]{1,0:T(8,128)} %refs_5_.1, f32[36,36]{1,0:T(8,128)} %refs_6_.1), custom_call_target="tpu_custom_call" | custom-call | tf_op jit(solution)/shard_map/pallas_call | solution.py:392
  22.9 38.2 %shard_map.105 = (f32[2304,128]{1,0:T(8,128)}, f32[4,768]{1,0:T(4,128)}) custom-call(s32[8,768]{1,0:T(8,128)} %bitcast.9, f32[8,768]{1,0:T(8,128)} %bitcast.10, f32[6,64,128]{2,1,0:T(8,128)} %get-tuple-element.6.surfaces, f32[2304,128]{1,0:T(8,128)} %get-tuple-element.7.field), custom_call_target="tpu_custom_call" | custom-call | tf_op jit(solution)/shard_map/pallas_call | solution.py:417

commit v4 on v3

--- a/solution.py
+++ b/solution.py
@@ -301,7 +301,7 @@
     own.wait()
 
 
-def gather_body(dims, cells, weights, surfaces, field, field_out, sensed, table, copy_sem, table_sem):
+def gather_body(dims, cells, weights, surfaces, field, field_out, sensed, table, held, load_sem, store_sem, table_sem):
     width, adjoints, n_t, n_s = dims
     lanes = table.shape[2]
     nx, ny = min(3, n_t), min(3, n_s)
@@ -310,12 +310,12 @@
     arrival = pltpu.make_async_copy(surfaces, table, table_sem)
     arrival.start()
     share = field.shape[0] // adjoints
-    copies = []
+    loads, stores = [], []
     for a in range(adjoints):
         rows = pl.ds(a * share, share)
-        copy = pltpu.make_async_copy(field.at[rows], field_out.at[rows], copy_sem.at[a])
-        copy.start()
-        copies.append(copy)
+        loads.append(pltpu.make_async_copy(field.at[rows], held.at[rows], load_sem.at[a]))
+        stores.append(pltpu.make_async_copy(held.at[rows], field_out.at[rows], store_sem.at[a]))
+        loads[a].start()
 
     column, row = divmod_const(cells[...], n_s * lanes)
     tile, in_tile = divmod_const(column, width)
@@ -347,13 +347,17 @@
         return tuple(taken)
 
     empty = jnp.zeros((slots, lanes), jnp.float32)
-    taken = lax.fori_loop(0, nx * ny * width, pick, (empty,) * (adjoints * chunks), unroll=4)
+    taken = lax.fori_loop(0, width, pick, (empty,) * (adjoints * chunks), unroll=4)
+    for load, store in zip(loads, stores):
+        load.wait()
+        store.start()
+    taken = lax.fori_loop(width, nx * ny * width, pick, taken, unroll=4)
     for a in range(adjoints):
         for c in range(chunks):
             part = taken[a * chunks + c] * weights[:, c * lanes : (c + 1) * lanes]
             sensed[a : a + 1, c * lanes : (c + 1) * lanes] = jnp.sum(part, axis=0, keepdims=True)
-    for copy in copies:
-        copy.wait()
+    for store in stores:
+        store.wait()
 
 
 def body(
@@ -421,6 +425,8 @@
         out_specs=(anywhere, vmem),
         scratch_shapes=[
             pltpu.VMEM(table_shape.shape, jnp.float32),
+            pltpu.VMEM(field_shape.shape, jnp.float32),
+            pltpu.SemaphoreType.DMA((adjoints,)),
             pltpu.SemaphoreType.DMA((adjoints,)),
             pltpu.SemaphoreType.DMA,
         ],

time: 61.4 us -> 33.8 us (0.55)
  Pallas kernels: 60.5 us -> 32.9 us
    pallas_call x1, Pallas kernels: 38.2 us -> 10.7 us  [body(): pl.pallas_call(functools.partial(gather_body, (width, adjoints, n_t, n_s)...]
where the time goes in v4:
time: 33.8 us; the launch traced here: 33.6 us
  Pallas kernels  32.9 us (97%)
  between operations  0.64 us (2%)
    pallas_call x1, Pallas kernels, body(): pl.pallas_call(functools.partial(kernel_body, (levels, width, adjoints, n...  22.3 us
    pallas_call x1, Pallas kernels, body(): pl.pallas_call(functools.partial(gather_body, (width, adjoints, n_t, n_s)...  10.7 us

profile of v4, /device:TPU:0, one launch (start us, length us, event | category | flops | bytes accessed | tf_op | source)
XLA Modules:
  0.0 33.6 jit_solution(1195054328791050488)
XLA Ops:
  0.6 22.3 %shard_map.104 = (f32[2304,128]{1,0:T(8,128)}, f32[6,64,128]{2,1,0:T(8,128)}) custom-call(f32[16,128]{1,0:T(8,128)} %refs_0_.1, s32[16,128]{1,0:T(8,128)} %refs_1_.1, f32[576,128]{1,0:T(8,128)} %bitcast.6, f32[576,128]{1,0:T(8,128)} %bitcast.7, f32[576,128]{1,0:T(8,128)} %bitcast.8, f32[16,128]{1,0:T(8,128)} %refs_5_.1, f32[36,36]{1,0:T(8,128)} %refs_6_.1), custom_call_target="tpu_custom_call" | custom-call | tf_op jit(solution)/shard_map/pallas_call | solution.py:396
  22.9 10.7 %shard_map.105 = (f32[2304,128]{1,0:T(8,128)}, f32[4,768]{1,0:T(4,128)}) custom-call(s32[8,768]{1,0:T(8,128)} %bitcast.9, f32[8,768]{1,0:T(8,128)} %bitcast.10, f32[6,64,128]{2,1,0:T(8,128)} %get-tuple-element.6.surfaces, f32[2304,128]{1,0:T(8,128)} %get-tuple-element.7.field), custom_call_target="tpu_custom_call" | custom-call | tf_op jit(solution)/shard_map/pallas_call | solution.py:421

commit v5 on v4

--- a/solution.py
+++ b/solution.py
@@ -327,35 +327,36 @@
     step_s = jnp.where(step_s < 0, step_s + ny, step_s)
     table_row = (step_t * ny + step_s) * width + in_tile
     elements = cells.shape[1]
-    chunks = elements // lanes
     slots = cells.shape[0]
+    chunk = 2 * lanes if elements % (2 * lanes) == 0 else lanes
+    lane_of = lax.broadcasted_iota(jnp.int32, (lanes, chunk), 0)
+    row_of = lax.broadcasted_iota(jnp.int32, (nx * ny * width, chunk), 0)
 
     arrival.wait()
-
-    def pick(at, carry):
-        slot, x = divmod_const(at, width)
-        taken = list(carry)
-        masks = [table_row[:, c * lanes : (c + 1) * lanes] == at for c in range(chunks)]
+    surface = table[...].reshape(nx * ny * adjoints * width, lanes)
+    high, low = split(surface)
+    surface = jnp.concatenate([high, low], axis=1).astype(jnp.bfloat16)
+
+    for c in range(elements // chunk):
+        span = slice(c * chunk, (c + 1) * chunk)
+        totals = [jnp.zeros((8, chunk), jnp.float32)] * adjoints
+        for k in range(slots):
+            chosen = jnp.where(lane_of == in_block[k : k + 1, span], 1.0, 0.0).astype(jnp.bfloat16)
+            chosen = jnp.concatenate([chosen, chosen], axis=0)
+            lines = jnp.dot(surface, chosen, preferred_element_type=jnp.float32)
+            share_of = jnp.where(row_of == table_row[k : k + 1, span], weights[k : k + 1, span], 0.0)
+            for a in range(adjoints):
+                for block in range(nx * ny):
+                    for x in range(0, width, 8):
+                        line = (block * adjoints + a) * width + x
+                        mine = block * width + x
+                        totals[a] += lines[line : line + 8] * share_of[mine : mine + 8]
         for a in range(adjoints):
-            line = jnp.broadcast_to(table[slot, pl.ds(a * width + x, 1), :], (slots, lanes))
-            for c in range(chunks):
-                found = jnp.take_along_axis(
-                    line, in_block[:, c * lanes : (c + 1) * lanes], axis=1, mode="promise_in_bounds"
-                )
-                i = a * chunks + c
-                taken[i] = jnp.where(masks[c], found, taken[i])
-        return tuple(taken)
-
-    empty = jnp.zeros((slots, lanes), jnp.float32)
-    taken = lax.fori_loop(0, width, pick, (empty,) * (adjoints * chunks), unroll=4)
-    for load, store in zip(loads, stores):
-        load.wait()
-        store.start()
-    taken = lax.fori_loop(width, nx * ny * width, pick, taken, unroll=4)
-    for a in range(adjoints):
-        for c in range(chunks):
-            part = taken[a * chunks + c] * weights[:, c * lanes : (c + 1) * lanes]
-            sensed[a : a + 1, c * lanes : (c + 1) * lanes] = jnp.sum(part, axis=0, keepdims=True)
+            sensed[a : a + 1, span] = jnp.sum(totals[a], axis=0, keepdims=True)
+        if c == 0:
+            for load, store in zip(loads, stores):
+                load.wait()
+                store.start()
     for store in stores:
         store.wait()
 

time: 33.8 us -> 27.7 us (0.82)
  Pallas kernels: 32.9 us -> 26.8 us
    pallas_call x1, Pallas kernels: 10.7 us -> 4.54 us  [body(): pl.pallas_call(functools.partial(gather_body, (width, adjoints, n_t, n_s)...]
where the time goes in v5:
time: 27.7 us; the launch traced here: 27.4 us
  Pallas kernels  26.8 us (97%)
  between operations  0.64 us (2%)
    pallas_call x1, Pallas kernels, body(): pl.pallas_call(functools.partial(kernel_body, (levels, width, adjoints, n...  22.3 us
    pallas_call x1, Pallas kernels, body(): pl.pallas_call(functools.partial(gather_body, (width, adjoints, n_t, n_s)...  4.54 us

profile of v5, /device:TPU:0, one launch (start us, length us, event | category | flops | bytes accessed | tf_op | source)
XLA Modules:
  0.0 27.4 jit_solution(13487417787383220851)
XLA Ops:
  0.6 22.3 %shard_map.104 = (f32[2304,128]{1,0:T(8,128)}, f32[6,64,128]{2,1,0:T(8,128)}) custom-call(f32[16,128]{1,0:T(8,128)} %refs_0_.1, s32[16,128]{1,0:T(8,128)} %refs_1_.1, f32[576,128]{1,0:T(8,128)} %bitcast.6, f32[576,128]{1,0:T(8,128)} %bitcast.7, f32[576,128]{1,0:T(8,128)} %bitcast.8, f32[16,128]{1,0:T(8,128)} %refs_5_.1, f32[36,36]{1,0:T(8,128)} %refs_6_.1), custom_call_target="tpu_custom_call" | custom-call | tf_op jit(solution)/shard_map/pallas_call | solution.py:397
  22.9 4.5 %shard_map.105 = (f32[2304,128]{1,0:T(8,128)}, f32[4,768]{1,0:T(4,128)}) custom-call(s32[8,768]{1,0:T(8,128)} %bitcast.9, f32[8,768]{1,0:T(8,128)} %bitcast.10, f32[6,64,128]{2,1,0:T(8,128)} %get-tuple-element.6.surfaces, f32[2304,128]{1,0:T(8,128)} %get-tuple-element.7.field), custom_call_target="tpu_custom_call" | custom-call | tf_op jit(solution)/shard_map/pallas_call | solution.py:422

commit v6 on v4

--- a/solution.py
+++ b/solution.py
@@ -44,9 +44,9 @@
     dims,
     *refs,
 ):
-    sources, (field, surfaces), scratch = refs[:7], refs[7:9], refs[9:]
-    arrivals, scratch = scratch[:7], scratch[7:]
-    innovation, cluster, kernel, wind_x, wind_y, strength, matrix = arrivals
+    sources, (field, sensed), scratch = refs[:9], refs[9:11], refs[11:]
+    arrivals, scratch = scratch[:9], scratch[9:]
+    innovation, cluster, kernel, wind_x, wind_y, strength, matrix, cells, weights = arrivals
     (
         base,
         face_x,
@@ -57,6 +57,8 @@
         table,
         held,
         square,
+        columns,
+        shares,
         send_sem,
         recv_sem,
         load_sem,
@@ -83,7 +85,7 @@
         pltpu.make_async_copy(source, arrival, load_sem.at[i])
         for i, (source, arrival) in enumerate(zip(sources, arrivals))
     ]
-    for i in (6, 2, 0, 1, 5, 3, 4):
+    for i in (6, 2, 0, 1, 5, 3, 4, 7, 8):
         loads[i].start()
 
     count = [0]
@@ -161,6 +163,23 @@
             there = slot_of(-dt, n_t) * ny + slot_of(-ds, n_s)
             copy = send(pack_a.at[0], pack_a.at[there], dt, ds)
             (far if dt else near).append(copy)
+    loads[7].wait()
+    loads[8].wait()
+    column, row = divmod_const(cells[...], n_s * lanes)
+    tile, in_tile = divmod_const(column, width)
+    block, in_block = divmod_const(row, lanes)
+    step_t = tile - me_t
+    step_t = jnp.where(step_t < 0, step_t + n_t, step_t)
+    step_t = jnp.where(step_t > 1, 2, step_t)
+    step_s = block - me_s
+    step_s = jnp.where(step_s < 0, step_s + ny, step_s)
+    table_row = (step_t * ny + step_s) * width + in_tile
+    slots, elements = cells.shape
+    lane_of = lax.broadcasted_iota(jnp.int32, (lanes, elements), 0)
+    row_of = lax.broadcasted_iota(jnp.int32, (nx * ny * width, elements), 0)
+    for k in range(slots):
+        columns[k] = jnp.where(lane_of == in_block[k : k + 1], 1.0, 0.0).astype(jnp.bfloat16)
+
     for copy in near:
         copy.wait()
 
@@ -240,6 +259,8 @@
         copy.wait()
     advance(-1, merged(pack_a, -1), width - 1)
     advance(width, merged(pack_a, 1), 0)
+    for k in range(slots):
+        shares[k] = jnp.where(row_of == table_row[k : k + 1], weights[k : k + 1], 0.0)
     for copy in copies:
         copy.wait()
     seam_b = merged(pack_b, 0)
@@ -284,31 +305,51 @@
             stores.append(copy)
 
     transport(0, 8)
-    copies = []
-    for dt, ds in partners:
+    near, far = [], []
+    for dt, ds in sorted(partners, key=lambda partner: partner[0] == 0):
         there = slot_of(-dt, n_t) * ny + slot_of(-ds, n_s)
-        copies.append(send(table.at[0], table.at[there], dt, ds))
+        (far if dt else near).append(send(table.at[0], table.at[there], dt, ds))
     store(0, 8)
     for low in range(8, padded, 8):
         transport(low, low + 8)
         store(low, low + 8)
-    for copy in copies:
-        copy.wait()
-    own = pltpu.make_async_copy(table, surfaces, store_sem.at[len(stores)])
-    own.start()
+
+    chunk = 2 * lanes if elements % (2 * lanes) == 0 else lanes
+
+    def gather(blocks, start):
+        surface = table[blocks[0] : blocks[-1] + 1].reshape(len(blocks) * adjoints * width, lanes)
+        surface = jnp.concatenate(split(surface), axis=1).astype(jnp.bfloat16)
+        for c in range(elements // chunk):
+            span = slice(c * chunk, (c + 1) * chunk)
+            totals = [jnp.zeros((8, chunk), jnp.float32)] * adjoints
+            for k in range(slots):
+                chosen = columns[k, :, span]
+                chosen = jnp.concatenate([chosen, chosen], axis=0)
+                lines = jnp.dot(surface, chosen, preferred_element_type=jnp.float32)
+                for a in range(adjoints):
+                    for i, block in enumerate(blocks):
+                        for x in range(0, width, 8):
+                            line = (i * adjoints + a) * width + x
+                            mine = block * width + x
+                            totals[a] += lines[line : line + 8] * shares[k, mine : mine + 8, span]
+            for a in range(adjoints):
+                part = jnp.sum(totals[a], axis=0, keepdims=True)
+                if not start:
+                    part = part + sensed[a : a + 1, span]
+                sensed[a : a + 1, span] = part
+
+    for copy in near:
+        copy.wait()
+    gather(range(ny), True)
+    for copy in far:
+        copy.wait()
+    gather(range(ny, nx * ny), False)
     for copy in stores:
         copy.wait()
-    own.wait()
-
-
-def gather_body(dims, cells, weights, surfaces, field, field_out, sensed, table, held, load_sem, store_sem, table_sem):
-    width, adjoints, n_t, n_s = dims
-    lanes = table.shape[2]
-    nx, ny = min(3, n_t), min(3, n_s)
-    me_t = lax.axis_index("tiles")
-    me_s = lax.axis_index("sub")
-    arrival = pltpu.make_async_copy(surfaces, table, table_sem)
-    arrival.start()
+
+
+def pass_body(adjoints, field, sensed, field_out, sensed_out, held, load_sem, store_sem):
+    sensed_out[...] = sensed[...]
     share = field.shape[0] // adjoints
     loads, stores = [], []
     for a in range(adjoints):
@@ -316,46 +357,9 @@
         loads.append(pltpu.make_async_copy(field.at[rows], held.at[rows], load_sem.at[a]))
         stores.append(pltpu.make_async_copy(held.at[rows], field_out.at[rows], store_sem.at[a]))
         loads[a].start()
-
-    column, row = divmod_const(cells[...], n_s * lanes)
-    tile, in_tile = divmod_const(column, width)
-    block, in_block = divmod_const(row, lanes)
-    step_t = tile - me_t
-    step_t = jnp.where(step_t < 0, step_t + n_t, step_t)
-    step_t = jnp.where(step_t > 1, 2, step_t)
-    step_s = block - me_s
-    step_s = jnp.where(step_s < 0, step_s + ny, step_s)
-    table_row = (step_t * ny + step_s) * width + in_tile
-    elements = cells.shape[1]
-    chunks = elements // lanes
-    slots = cells.shape[0]
-
-    arrival.wait()
-
-    def pick(at, carry):
-        slot, x = divmod_const(at, width)
-        taken = list(carry)
-        masks = [table_row[:, c * lanes : (c + 1) * lanes] == at for c in range(chunks)]
-        for a in range(adjoints):
-            line = jnp.broadcast_to(table[slot, pl.ds(a * width + x, 1), :], (slots, lanes))
-            for c in range(chunks):
-                found = jnp.take_along_axis(
-                    line, in_block[:, c * lanes : (c + 1) * lanes], axis=1, mode="promise_in_bounds"
-                )
-                i = a * chunks + c
-                taken[i] = jnp.where(masks[c], found, taken[i])
-        return tuple(taken)
-
-    empty = jnp.zeros((slots, lanes), jnp.float32)
-    taken = lax.fori_loop(0, width, pick, (empty,) * (adjoints * chunks), unroll=4)
     for load, store in zip(loads, stores):
         load.wait()
         store.start()
-    taken = lax.fori_loop(width, nx * ny * width, pick, taken, unroll=4)
-    for a in range(adjoints):
-        for c in range(chunks):
-            part = taken[a * chunks + c] * weights[:, c * lanes : (c + 1) * lanes]
-            sensed[a : a + 1, c * lanes : (c + 1) * lanes] = jnp.sum(part, axis=0, keepdims=True)
     for store in stores:
         store.wait()
 
@@ -390,14 +394,16 @@
         wind_y.reshape(levels * width, lanes),
         conv_strength,
         conv_matrix,
+        margin_cell.T,
+        margin_weight.T,
     )
     field_shape = jax.ShapeDtypeStruct((adjoints * levels * width, lanes), jnp.float32)
-    table_shape = jax.ShapeDtypeStruct((nx * ny, adjoints * width, lanes), jnp.float32)
-    field, surfaces = pl.pallas_call(
+    sensed_shape = jax.ShapeDtypeStruct((adjoints, elements), jnp.float32)
+    field, sensed = pl.pallas_call(
         functools.partial(kernel_body, (levels, width, adjoints, n_t, n_s)),
-        out_shape=(field_shape, table_shape),
+        out_shape=(field_shape, sensed_shape),
         in_specs=[anywhere] * len(operands),
-        out_specs=(anywhere, anywhere),
+        out_specs=(anywhere, vmem),
         scratch_shapes=[pltpu.VMEM(x.shape, x.dtype) for x in operands]
         + [
             pltpu.VMEM((width + 4, padded, lanes), jnp.float32),
@@ -406,32 +412,32 @@
             pltpu.VMEM((nx * ny, padded, lanes), jnp.float32),
             pltpu.VMEM((ny, padded, lanes), jnp.float32),
             pltpu.VMEM((width + 2, adjoints, padded, lanes), jnp.float32),
-            pltpu.VMEM(table_shape.shape, jnp.float32),
+            pltpu.VMEM((nx * ny, adjoints * width, lanes), jnp.float32),
             pltpu.VMEM(field_shape.shape, jnp.float32),
             pltpu.VMEM((depth, depth), jnp.float32),
+            pltpu.VMEM((slots, lanes, elements), jnp.bfloat16),
+            pltpu.VMEM((slots, nx * ny * width, elements), jnp.float32),
             pltpu.SemaphoreType.DMA((n_sems,)),
             pltpu.SemaphoreType.DMA((n_sems,)),
             pltpu.SemaphoreType.DMA((len(operands),)),
-            pltpu.SemaphoreType.DMA((adjoints * padded // 8 + 1,)),
+            pltpu.SemaphoreType.DMA((adjoints * padded // 8,)),
         ],
         compiler_params=pltpu.CompilerParams(
             collective_id=0, has_side_effects=True, vmem_limit_bytes=limit
         ),
     )(*operands)
     field, sensed = pl.pallas_call(
-        functools.partial(gather_body, (width, adjoints, n_t, n_s)),
-        out_shape=(field_shape, jax.ShapeDtypeStruct((adjoints, elements), jnp.float32)),
-        in_specs=[vmem, vmem, anywhere, anywhere],
+        functools.partial(pass_body, adjoints),
+        out_shape=(field_shape, sensed_shape),
+        in_specs=[anywhere, vmem],
         out_specs=(anywhere, vmem),
         scratch_shapes=[
-            pltpu.VMEM(table_shape.shape, jnp.float32),
             pltpu.VMEM(field_shape.shape, jnp.float32),
             pltpu.SemaphoreType.DMA((adjoints,)),
             pltpu.SemaphoreType.DMA((adjoints,)),
-            pltpu.SemaphoreType.DMA,
         ],
         compiler_params=pltpu.CompilerParams(vmem_limit_bytes=limit),
-    )(margin_cell.T, margin_weight.T, surfaces, field)
+    )(field, sensed)
     return field.reshape(adjoints, levels, width, lanes), sensed
 
 

time: 33.8 us -> 27.4 us (0.81)
  Pallas kernels: 32.9 us -> 26.6 us
    pallas_call x1, Pallas kernels: 10.7 us -> 3.34 us  [body(): pl.pallas_call(functools.partial(pass_body, adjoints), out_shape=(field_s...]
    pallas_call x1, Pallas kernels: 22.3 us -> 23.2 us  [body(): pl.pallas_call(functools.partial(kernel_body, (levels, width, adjoints, n...]
where the time goes in v6:
time: 27.4 us; the launch traced here: 27.2 us
  Pallas kernels  26.6 us (97%)
  between operations  0.64 us (2%)
    pallas_call x1, Pallas kernels, body(): pl.pallas_call(functools.partial(kernel_body, (levels, width, adjoints, n...  23.2 us
    pallas_call x1, Pallas kernels, body(): pl.pallas_call(functools.partial(pass_body, adjoints), out_shape=(field_s...  3.34 us

profile of v6, /device:TPU:0, one launch (start us, length us, event | category | flops | bytes accessed | tf_op | source)
XLA Modules:
  0.0 27.2 jit_solution(2665205868242048536)
XLA Ops:
  0.6 23.2 %shard_map.104 = (f32[2304,128]{1,0:T(8,128)}, f32[4,768]{1,0:T(4,128)}) custom-call(f32[16,128]{1,0:T(8,128)} %refs_0_.1, s32[16,128]{1,0:T(8,128)} %refs_1_.1, f32[576,128]{1,0:T(8,128)} %bitcast.6, f32[576,128]{1,0:T(8,128)} %bitcast.7, f32[576,128]{1,0:T(8,128)} %bitcast.8, f32[16,128]{1,0:T(8,128)} %refs_5_.1, f32[36,36]{1,0:T(8,128)} %refs_6_.1, ...), custom_call_target="tpu_custom_call" | custom-call | tf_op jit(solution)/shard_map/pallas_call | solution.py:402
  23.9 3.3 %shard_map.105 = (f32[2304,128]{1,0:T(8,128)}, f32[4,768]{1,0:T(4,128)}) custom-call(f32[2304,128]{1,0:T(8,128)} %get-tuple-element.6.field, f32[4,768]{1,0:T(4,128)} %get-tuple-element.7.sensed), custom_call_target="tpu_custom_call" | custom-call | tf_op jit(solution)/shard_map/pallas_call | solution.py:429

commit v7 on v6

--- a/solution.py
+++ b/solution.py
@@ -348,15 +348,16 @@
         copy.wait()
 
 
-def pass_body(adjoints, field, sensed, field_out, sensed_out, held, load_sem, store_sem):
-    sensed_out[...] = sensed[...]
-    share = field.shape[0] // adjoints
-    loads, stores = [], []
-    for a in range(adjoints):
-        rows = pl.ds(a * share, share)
-        loads.append(pltpu.make_async_copy(field.at[rows], held.at[rows], load_sem.at[a]))
-        stores.append(pltpu.make_async_copy(held.at[rows], field_out.at[rows], store_sem.at[a]))
-        loads[a].start()
+def pass_body(parts, field, sensed, field_out, sensed_out, field_held, sensed_held, load_sem, store_sem):
+    share = field.shape[0] // parts
+    pieces = [pl.ds(part * share, share) for part in range(parts)]
+    loads = [(field.at[piece], field_held.at[piece]) for piece in pieces] + [(sensed, sensed_held)]
+    stores = [(field_held.at[piece], field_out.at[piece]) for piece in pieces]
+    stores.append((sensed_held, sensed_out))
+    loads = [pltpu.make_async_copy(*ends, load_sem.at[i]) for i, ends in enumerate(loads)]
+    stores = [pltpu.make_async_copy(*ends, store_sem.at[i]) for i, ends in enumerate(stores)]
+    for load in loads:
+        load.start()
     for load, store in zip(loads, stores):
         load.wait()
         store.start()
@@ -426,15 +427,17 @@
             collective_id=0, has_side_effects=True, vmem_limit_bytes=limit
         ),
     )(*operands)
+    parts = 2 * adjoints
     field, sensed = pl.pallas_call(
-        functools.partial(pass_body, adjoints),
+        functools.partial(pass_body, parts),
         out_shape=(field_shape, sensed_shape),
-        in_specs=[anywhere, vmem],
-        out_specs=(anywhere, vmem),
+        in_specs=[anywhere, anywhere],
+        out_specs=(anywhere, anywhere),
         scratch_shapes=[
             pltpu.VMEM(field_shape.shape, jnp.float32),
-            pltpu.SemaphoreType.DMA((adjoints,)),
-            pltpu.SemaphoreType.DMA((adjoints,)),
+            pltpu.VMEM(sensed_shape.shape, jnp.float32),
+            pltpu.SemaphoreType.DMA((parts + 1,)),
+            pltpu.SemaphoreType.DMA((parts + 1,)),
         ],
         compiler_params=pltpu.CompilerParams(vmem_limit_bytes=limit),
     )(field, sensed)

time: 27.4 us -> 26.2 us (0.956)
  Pallas kernels: 26.6 us -> 25.4 us
    pallas_call x1, Pallas kernels: 3.34 us -> 2.17 us  [body(): pl.pallas_call(functools.partial(pass_body, parts), out_shape=(field_shap...]
where the time goes in v7:
time: 26.2 us; the launch traced here: 26 us
  Pallas kernels  25.4 us (97%)
  between operations  0.64 us (2%)
    pallas_call x1, Pallas kernels, body(): pl.pallas_call(functools.partial(kernel_body, (levels, width, adjoints, n...  23.2 us
    pallas_call x1, Pallas kernels, body(): pl.pallas_call(functools.partial(pass_body, parts), out_shape=(field_shap...  2.17 us

profile of v7, /device:TPU:0, one launch (start us, length us, event | category | flops | bytes accessed | tf_op | source)
XLA Modules:
  0.0 26.0 jit_solution(7622953300640347787)
XLA Ops:
  0.6 23.2 %shard_map.104 = (f32[2304,128]{1,0:T(8,128)}, f32[4,768]{1,0:T(4,128)}) custom-call(f32[16,128]{1,0:T(8,128)} %refs_0_.1, s32[16,128]{1,0:T(8,128)} %refs_1_.1, f32[576,128]{1,0:T(8,128)} %bitcast.6, f32[576,128]{1,0:T(8,128)} %bitcast.7, f32[576,128]{1,0:T(8,128)} %bitcast.8, f32[16,128]{1,0:T(8,128)} %refs_5_.1, f32[36,36]{1,0:T(8,128)} %refs_6_.1, ...), custom_call_target="tpu_custom_call" | custom-call | tf_op jit(solution)/shard_map/pallas_call | solution.py:403
  23.9 2.2 %shard_map.105 = (f32[2304,128]{1,0:T(8,128)}, f32[4,768]{1,0:T(4,128)}) custom-call(f32[2304,128]{1,0:T(8,128)} %get-tuple-element.6.field, f32[4,768]{1,0:T(4,128)} %get-tuple-element.7.sensed), custom_call_target="tpu_custom_call" | custom-call | tf_op jit(solution)/shard_map/pallas_call | solution.py:431
